TPU v7x, 256 devices: a whole 4x4x8 slice. The times are simulated.
256 devices in a mesh: peer: 16 (over z_hi, x), fsdp: 16 (over y, z_lo, core).
Axes of the slice: x: 4, y: 4, z: 8 (z_hi: 4, z_lo: 2; z = z_hi * 2 + z_lo), core: 2. Of those that a mesh axis runs over, the one named last changes fastest.
Arguments:
- tokens: bfloat16 [65536, 4608], P(('peer', 'fsdp')), may hold values from -6 to 6
- cotangent: bfloat16 [65536, 1024], P(('peer', 'fsdp')), may hold values from -6 to 6
- weight: float32 [16, 4608, 1024], P('peer', 'fsdp'), may hold values from -4 to 4
- first_moment: float32 [16, 4608, 1024], P('peer', 'fsdp'), may hold values from -3 to 3
- second_moment: float32 [16, 4608, 1024], P('peer', 'fsdp'), may hold values from 0.25 to 4
- step: int32 [1], replicated, may hold values from 0 to 2999
Outputs:
- values: bfloat16 [65536, 1024], P(('peer', 'fsdp'))
- new_weight: float32 [16, 4608, 1024], P('peer', 'fsdp')
- new_first: float32 [16, 4608, 1024], P('peer', 'fsdp')
- new_second: float32 [16, 4608, 1024], P('peer', 'fsdp')
All inputs are finite; a program needn't handle non-finite values.
Results may differ from a plain program's by a relative error of at most 0.0057.
Values may be sent and summed in bfloat16 or wider, within the bound.
No kernel may reach another device: no remote copies, remote signals or barrier semaphores. Data moves between devices by JAX's collectives and lax.ppermute only.
A program may use at most 128 MiB of HBM per device.

v0:
```python
from functools import partial

import jax
import jax.numpy as jnp
from jax import lax
from jax.experimental import pallas as pl
from jax.experimental.pallas import tpu as pltpu
from jax.sharding import PartitionSpec as P

D = 4608
Y, Z, C = 4, 2, 2
BF, F32 = jnp.bfloat16, jnp.float32
MIB = 2**20


def hop(value, dy=0, dz=0, dc=0):
    pairs = []
    for i in range(Y * Z * C):
        y, z, c = i // (Z * C), i // C % Z, i % C
        pairs.append((i, ((y + dy) % Y * Z + (z ^ dz)) * C + (c ^ dc)))
    return lax.ppermute(value, "fsdp", pairs)


def gossip(value, bit):
    mask = 2**bit
    pairs = [(source, source ^ mask) for source in range(lax.axis_size("peer"))]
    return lax.ppermute(value, "peer", pairs)


def where():
    index = lax.axis_index("fsdp")
    return index // (Z * C), index // C % Z, index % C


def pick(bit, first, second):
    return jnp.where(bit == 0, first, second)


def after(values, *earlier):
    return lax.optimization_barrier(tuple(values) + earlier)[: len(values)]


def shape(dtype, *dims):
    return jax.ShapeDtypeStruct(dims, dtype)


def kernel_call(kernel, ins, outs, scratch=(), limit=16, flops=0):
    moved = sum(a.size * a.dtype.itemsize for a in (*ins, *outs))
    return pl.pallas_call(
        kernel,
        in_specs=[pl.BlockSpec(memory_space=pltpu.VMEM)] * len(ins),
        out_specs=[pl.BlockSpec(memory_space=pltpu.VMEM)] * len(outs),
        out_shape=list(outs),
        scratch_shapes=list(scratch),
        compiler_params=pltpu.CompilerParams(vmem_limit_bytes=limit * MIB),
        cost_estimate=pl.CostEstimate(flops=flops, bytes_accessed=moved, transcendentals=0),
    )(*ins)


def dot(left, right):
    return jnp.dot(left, right, preferred_element_type=F32)


def dot_rows(left, right):
    return lax.dot_general(left, right, (((0,), (0,)), ((), ())), preferred_element_type=F32)


def norm_kernel(tokens, norm_2, norm_r, rows, sems):
    y, _, _ = where()
    width, tile = norm_2.shape[1], rows.shape[1]
    copies = [
        pltpu.make_async_copy(tokens.at[pl.ds(t * tile, tile), :], rows.at[t], sems.at[t])
        for t in range(rows.shape[0])
    ]
    for copy in copies:
        copy.start()
    for t, copy in enumerate(copies):
        here = slice(t * tile, (t + 1) * tile)
        copy.wait()
        squares = 0.0
        for i in range(tokens.shape[1] // 128):
            part = rows[t, :, i * 128 : (i + 1) * 128].astype(F32)
            squares += part * part
        scale = lax.rsqrt(jnp.sum(squares, axis=1, keepdims=True) / D + 1e-06)
        for slot, k in enumerate((2, 1, 3, 0)):
            start = pl.multiple_of(lax.rem(y + k, Y) * width, 128)
            part = (rows[t, :, pl.ds(start, width)].astype(F32) * scale).astype(BF)
            if slot == 0:
                norm_2[here, :] = part
            else:
                norm_r[slot - 1, here, :] = part


def normalise(tokens):
    count, width = tokens.shape[0], tokens.shape[1] // Y
    tiles = 8
    return pl.pallas_call(
        norm_kernel,
        in_specs=[pl.BlockSpec(memory_space=pl.ANY)],
        out_specs=[pl.BlockSpec(memory_space=pltpu.VMEM)] * 2,
        out_shape=[shape(BF, count, width), shape(BF, 3, count, width)],
        scratch_shapes=[
            pltpu.VMEM((tiles, count // tiles, tokens.shape[1]), BF),
            pltpu.SemaphoreType.DMA((tiles,)),
        ],
        compiler_params=pltpu.CompilerParams(vmem_limit_bytes=12 * MIB),
        cost_estimate=pl.CostEstimate(flops=0, bytes_accessed=4 * tokens.size, transcendentals=0),
    )(tokens)


def term(mine, theirs, cot_mine, cot_theirs, product):
    width = mine.shape[1]
    tile = width // 3
    for i in range(3):
        here = slice(i * tile, (i + 1) * tile)
        product[here, :] = (
            dot_rows(mine[:, here], cot_mine[...]) + dot_rows(theirs[:, here], cot_theirs[...])
        ).astype(BF)


def term_2_kernel(mine, theirs, cot_mine, cot_theirs, low, high, near, far, product):
    (_, z, _), tall, quarter = where(), low.shape[0], low.shape[1]
    term(mine, theirs, cot_mine, cot_theirs, product)
    low[...] = product[:tall, :quarter]
    high[...] = product[tall:, :quarter]
    near[...] = pick(z, product[:tall, quarter:], product[tall:, quarter:])
    far[...] = pick(z, product[tall:, quarter:], product[:tall, quarter:])


def term_r_kernel(mine, theirs, cot_mine, cot_theirs, part_a, near, far, product):
    (_, z, _), tall, quarter = where(), near.shape[1], near.shape[2]

    def step(k, carry):
        term(mine.at[k], theirs.at[k], cot_mine, cot_theirs, product)
        part_a[k] = product[:, :quarter]
        near[k] = pick(z, product[:tall, quarter:], product[tall:, quarter:])
        far[k] = pick(z, product[tall:, quarter:], product[:tall, quarter:])
        return carry

    lax.fori_loop(0, 3, step, 0)


def scatter_2_kernel(part_a, low, high, near, got, up, down):
    tall = low.shape[0]
    wide, mid = 2 * tall, tall // 2
    up[:tall] = part_a[0, :tall] + low[...]
    up[tall:wide] = part_a[0, tall:]
    up[wide:] = near[:mid] + got[:mid]
    down[:tall] = part_a[1, :tall]
    down[tall:wide] = part_a[1, tall:] + high[...]
    down[wide:] = near[mid:] + got[mid:]


def scatter_3_kernel(part_a, near, below, above, got, up, down, far_a, near_a, sum_b, total):
    (_, z, _), tall = where(), far_a.shape[0]
    wide, mid = 2 * tall, tall // 2
    up[:mid] = near[0, :mid] + got[0, :mid] + below[wide:]
    up[mid:] = near[0, mid:] + got[0, mid:]
    down[:mid] = near[1, :mid] + got[1, :mid]
    down[mid:] = near[1, mid:] + got[1, mid:] + above[wide:]
    sum_b[...] = near[2].astype(F32) + got[2].astype(F32)
    total[...] = part_a[2].astype(F32) + below[:wide].astype(F32) + above[:wide].astype(F32)
    near_a[...] = pick(z, total[:tall], total[tall:])
    far_a[...] = pick(z, total[tall:], total[:tall]).astype(BF)


def scatter_4_kernel(near_a, last_z, sum_b, below, above, own, theirs, total):
    (_, _, c), rows, quarter = where(), own.shape[0], near_a.shape[1]
    total[:, :quarter] = near_a[...] + last_z[...].astype(F32)
    total[:, quarter:] = sum_b[...] + below[...].astype(F32) + above[...].astype(F32)
    own[...] = pick(c, total[:rows], total[rows:])
    theirs[...] = pick(c, total[rows:], total[:rows]).astype(BF)


def gather_1_kernel(mine, theirs, block_a, block_b):
    (_, _, c), rows, quarter = where(), mine.shape[0], block_a.shape[1]
    first, second = pick(c, mine[...], theirs[...]), pick(c, theirs[...], mine[...])
    block_a[:rows], block_b[:rows] = first[:, :quarter], first[:, quarter:]
    block_a[rows:], block_b[rows:] = second[:, :quarter], second[:, quarter:]


def gather_2_kernel(block_a, block_b, block_z, above, below, up, down, along):
    (_, z, _), tall = where(), block_a.shape[0]
    wide, mid = 2 * tall, tall // 2
    for out in (up, down):
        out[:tall] = pick(z, block_b[...], block_z[...])
        out[tall:wide] = pick(z, block_z[...], block_b[...])
    up[wide:] = below[:mid]
    down[wide:] = above[mid:]
    along[0] = above[...]
    along[1] = below[...]
    along[2] = block_a[...]


def gather_3_kernel(got_up, got_down, up, down, line):
    tall = line.shape[0]
    wide, mid = 2 * tall, tall // 2
    up[...] = got_up[:tall]
    down[...] = got_down[tall:wide]
    line[:mid] = got_up[wide:]
    line[mid:] = got_down[wide:]


def project(mine, theirs, whole, total):
    count = mine.shape[0]
    total[:count] += dot(mine, whole)
    total[count:] += dot(theirs, whole)


def order_z(z, own, other, whole):
    tall, quarter = own.shape
    whole[:tall, :quarter] = pick(z, own, other)
    whole[tall:, :quarter] = pick(z, other, own)


def project_r_kernel(mine, theirs, along, got_z, own_up, got_up, got_down, total, whole):
    _, z, _ = where()
    wide, quarter = whole.shape[0], got_up.shape[1]
    total[...] = jnp.zeros_like(total)
    for k, part in enumerate((got_down, got_up, own_up)):
        order_z(z, along[k], got_z[k], whole)
        whole[:, quarter:] = part[:wide]
        project(mine[k], theirs[k], whole[...], total)


def project_2_kernel(mine, theirs, line, got_z, low, high, before, own, other, whole, total):
    _, z, _ = where()
    tall, quarter = line.shape
    count = own.shape[0]
    order_z(z, line[...], got_z[...], whole)
    whole[:tall, quarter:] = low[...]
    whole[tall:, quarter:] = high[...]
    total[...] = before[...]
    project(mine[...], theirs[...], whole[...], total)
    own[...] = (total[:count] * D ** (-0.5)).astype(BF)
    other[...] = (total[count:] * D ** (-0.5)).astype(BF)


def place_kernel(own, other, values):
    (_, _, c), half = where(), own.shape[1]
    values[:, :half] = pick(c, own[...], other[...])
    values[:, half:] = pick(c, other[...], own[...])


def adam_kernel(rates, mine, other, master, first, second, new_first, new_second, updated, wire):
    (_, _, c), half = where(), mine.shape[1]

    def rows(i, carry):
        here = pl.ds(pl.multiple_of(i * 16, 16), 16)
        for j in range(2):
            there = slice(j * half, (j + 1) * half)
            grad = jnp.where(c == j, mine[here, :], other[here, :].astype(F32)) * D ** (-0.5)
            moment = 0.9 * first[0, here, there] + 0.1 * grad
            square = 0.999 * second[0, here, there] + 0.001 * grad * grad
            scaled = square * rates[1]
            root = scaled * lax.rsqrt(scaled) + 1e-08
            guess = pl.reciprocal(root, approx=True)
            change = moment * rates[0] * (guess * (2.0 - root * guess))
            old = master[0, here, there]
            result = old - 0.02 * (change + 0.1 * old)
            new_first[0, here, there] = moment
            new_second[0, here, there] = square
            updated[here, there] = result
            wire[here, there] = result.astype(BF)
        return carry

    lax.fori_loop(0, mine.shape[0] // 16, rows, 0, unroll=2)


def adam(step, mine, other, master, first, second):
    _, rows, cols = master.shape
    half, tile = cols // 2, rows // 3
    time = (step[0] + 1).astype(F32)
    rate_one = 1.0 - jnp.exp(time * jnp.log(F32(0.9)))
    rate_two = 1.0 - jnp.exp(time * jnp.log(F32(0.999)))
    rates = jnp.stack([1.0 / rate_one, 1.0 / rate_two])
    part = pl.BlockSpec((tile, half), lambda i: (i, 0))
    full = pl.BlockSpec((1, tile, cols), lambda i: (0, i, 0))
    flat = pl.BlockSpec((tile, cols), lambda i: (i, 0))
    scalar = pl.BlockSpec(memory_space=pltpu.SMEM)
    return pl.pallas_call(
        adam_kernel,
        grid=(3,),
        in_specs=[scalar, part, part, full, full, full],
        out_specs=[full, full, flat, flat],
        out_shape=[
            shape(F32, 1, rows, cols),
            shape(F32, 1, rows, cols),
            shape(F32, rows, cols),
            shape(BF, rows, cols),
        ],
        cost_estimate=pl.CostEstimate(flops=20 * rows * cols, bytes_accessed=30 * rows * cols, transcendentals=0),
    )(rates, mine, other, master, first, second)


def on_device(tokens, cotangent, weight, first_moment, second_moment, step):
    _, _, c = where()
    master = weight[0]
    rows, cols = master.shape
    half, quarter, tall = cols // 2, cols // 4, rows * C
    wide, mid = 2 * tall, tall // 2
    tokens_here = tokens.shape[0]

    cot_mine = lax.dynamic_slice_in_dim(cotangent, c * half, half, 1)
    cot_theirs = hop(lax.dynamic_slice_in_dim(cotangent, (1 - c) * half, half, 1), dc=1)
    norm_2, norm_r = normalise(tokens)
    far_2 = hop(norm_2, dc=1)

    block = shape(BF, tall, quarter)
    product = pltpu.VMEM((wide, half), BF)
    low, high, near_2, got_2 = kernel_call(
        term_2_kernel,
        (norm_2, far_2, cot_mine, cot_theirs),
        (block,) * 4,
        (product,),
        limit=12,
        flops=4 * tokens_here * wide * half,
    )
    (send_r,) = after((norm_r,), low)
    far_r = hop(send_r, dc=1)
    three = shape(BF, 3, tall, quarter)
    part_a, near_r, got_r = kernel_call(
        term_r_kernel,
        (norm_r, far_r, cot_mine, cot_theirs),
        (shape(BF, 3, wide, quarter), three, three),
        (product,),
        limit=20,
        flops=12 * tokens_here * wide * half,
    )

    theirs = lax.dynamic_slice_in_dim(master, (1 - c) * half, half, 1).astype(BF)
    mine = lax.dynamic_slice_in_dim(master, c * half, half, 1).astype(BF)
    (theirs,) = after((theirs,), low)
    theirs = hop(theirs, dc=1)
    block_a, block_b = kernel_call(gather_1_kernel, (mine, theirs), (block, block), limit=8)
    low = hop(low, dy=1)
    high = hop(high, dy=-1)
    got_2 = hop(got_2, dz=1)
    got_r = hop(got_r, dz=1)
    long = shape(BF, wide + mid, quarter)
    up, down = kernel_call(scatter_2_kernel, (part_a, low, high, near_2, got_2), (long, long))
    send_a, send_b = after((block_a, block_b), up, down)
    from_below = hop(up, dy=1)
    from_above = hop(down, dy=-1)
    above = hop(send_a, dy=-1)
    below = hop(send_a, dy=1)
    block_z = hop(send_b, dz=1)
    block_f = shape(F32, tall, quarter)
    up, down, far_a, near_a, sum_b = kernel_call(
        scatter_3_kernel,
        (part_a, near_r, from_below, from_above, got_r),
        (block, block, block, block_f, block_f),
        (pltpu.VMEM((wide, quarter), F32),),
    )
    last_below = hop(up, dy=1)
    last_above = hop(down, dy=-1)
    last_z = hop(far_a, dz=1)
    own, other = kernel_call(
        scatter_4_kernel,
        (near_a, last_z, sum_b, last_below, last_above),
        (shape(F32, rows, half), shape(BF, rows, half)),
        (pltpu.VMEM((tall, half), F32),),
        limit=12,
    )
    other = hop(other, dc=1)

    up, down, along = kernel_call(
        gather_2_kernel, (block_a, block_b, block_z, above, below), (long, long, three)
    )
    up, down, along = after((up, down, along), last_below, last_above, last_z)
    got_up = hop(up, dy=1)
    got_down = hop(down, dy=-1)
    got_z = hop(along, dz=1)
    new_first, new_second, updated, wire = adam(step, own, other, weight, first_moment, second_moment)
    levels = lax.axis_size("peer").bit_length() - 1
    partner = lax.switch(step[0] % levels, [partial(gossip, bit=which) for which in range(levels)], wire)
    got_up, got_down = after((got_up, got_down), partner)
    last_up, last_down, line = kernel_call(
        gather_3_kernel, (got_up, got_down), (block, block, block), limit=8
    )
    last_up = hop(last_up, dy=1)
    last_down = hop(last_down, dy=-1)
    line_z = hop(line, dz=1)

    whole = pltpu.VMEM((wide, half), BF)
    (total,) = kernel_call(
        project_r_kernel,
        (norm_r, far_r, along, got_z, up, got_up, got_down),
        (shape(F32, 2 * tokens_here, half),),
        (whole,),
        limit=20,
        flops=12 * tokens_here * wide * half,
    )
    result = shape(BF, tokens_here, half)
    result_own, result_other = kernel_call(
        project_2_kernel,
        (norm_2, far_2, line, line_z, last_up, last_down, total),
        (result, result),
        (whole, pltpu.VMEM((2 * tokens_here, half), F32)),
        limit=16,
        flops=4 * tokens_here * wide * half,
    )
    (values,) = kernel_call(
        place_kernel, (result_own, hop(result_other, dc=1)), (shape(BF, tokens_here, cols),), limit=8
    )

    averaged = 0.5 * (updated + partner.astype(F32))
    return (values, averaged[None], new_first, new_second)


def solution(mesh):
    return jax.shard_map(
        on_device,
        mesh=mesh,
        in_specs=(
            P(("peer", "fsdp"), None),
            P(("peer", "fsdp"), None),
            P("peer", "fsdp", None),
            P("peer", "fsdp", None),
            P("peer", "fsdp", None),
            P(),
        ),
        out_specs=(
            P(("peer", "fsdp"), None),
            P("peer", "fsdp", None),
            P("peer", "fsdp", None),
            P("peer", "fsdp", None),
        ),
        check_vma=False,
    )
```

profile of v0, /device:TPU:1, one launch (start us, length us, event | category | flops | bytes accessed | tf_op | source)
XLA Modules:
  0.0 118.2 jit_solution(5937467730818172699)
XLA Ops:
  0.6 1.7 %copy-done = bf16[256,4608]{1,0:T(8,128)(2,1)S(1)} copy-done((bf16[256,4608]{1,0:T(8,128)(2,1)S(1)}, bf16[256,4608]{1,0:T(8,128)(2,1)}, u32[]{:S(2)}) %copy-start) | copy-done | bytes 2359320
  2.3 1.9 %shard_map.93 = (bf16[256,1152]{1,0:T(8,128)(2,1)S(1)}, bf16[3,256,1152]{2,1,0:T(8,128)(2,1)S(1)}) custom-call(bf16[256,4608]{1,0:T(8,128)(2,1)S(1)} %copy-done), custom_call_target="tpu_custom_call" | custom-call | bytes 4718592 | tf_op jit(solution)/shard_map/pallas_call | solution.py:97
  4.2 3.3 %collective-permute-start.4 = (bf16[256,1152]{1,0:T(8,128)(2,1)S(1)}, bf16[256,1152]{1,0:T(8,128)(2,1)S(1)}, u32[]{:S(2)}, u32[]{:S(2)}) collective-permute-start(bf16[256,1152]{1,0:T(8,128)(2,1)S(1)} %get-tuple-element.54.mine), channel_id=1, source_target_pairs={{0,1},{1,0},{2,3},{3,2},{4,5},{5,4},{6,7},{7,6},{8,9},{9,8},{10,11... | collective-permute-start | bytes 1769480 | tf_op jit(solution)/shard_map/ppermute | solution.py:21
  7.6 0.1 collective-permute-start.5
  7.8 1.8 %collective-permute-done.5.cot_theirs = bf16[256,512]{1,0:T(8,128)(2,1)S(1)} collective-permute-done((bf16[256,512]{1,0:T(8,128)(2,1)S(1)}, bf16[256,512]{1,0:T(8,128)(2,1)S(1)}, u32[]{:S(2)}, u32[]{:S(2)}) %collective-permute-start.5) | collective-permute-done | bytes 262176 | tf_op jit(solution)/shard_map/ppermute | solution.py:21
  9.6 0.8 shard_map.94
  10.4 0.5 collective-permute-start.7
  10.9 1.2 %collective-permute-start.10 = (bf16[576,256]{1,0:T(8,128)(2,1)S(1)}, bf16[576,256]{1,0:T(8,128)(2,1)S(1)}, u32[]{:S(2)}, u32[]{:S(2)}) collective-permute-start(bf16[576,256]{1,0:T(8,128)(2,1)S(1)} %get-tuple-element.64), channel_id=1, source_target_pairs={{0,2},{1,3},{2,0},{3,1},{4,6},{5,7},{6,4},{7,5},{8,10},{9,11},{10,... | collective-permute-start | bytes 884744 | tf_op jit(solution)/shard_map/ppermute | solution.py:21
  12.1 1.5 %collective-permute-start.9 = (bf16[576,256]{1,0:T(8,128)(2,1)S(1)}, bf16[576,256]{1,0:T(8,128)(2,1)S(1)}, u32[]{:S(2)}, u32[]{:S(2)}) collective-permute-start(bf16[576,256]{1,0:T(8,128)(2,1)S(1)} %get-tuple-element.62), channel_id=1, source_target_pairs={{0,12},{1,13},{2,14},{3,15},{4,0},{5,1},{6,2},{7,3},{8,4},{9,5},{1... | collective-permute-start | bytes 884744 | tf_op jit(solution)/shard_map/ppermute | solution.py:21
  13.5 0.6 collective-permute-done.7.theirs
  14.2 2.4 %shard_map.96 = (bf16[3,1152,256]{2,1,0:T(8,128)(2,1)S(1)}, bf16[3,576,256]{2,1,0:T(8,128)(2,1)S(1)}, bf16[3,576,256]{2,1,0:T(8,128)(2,1)S(1)}) custom-call(bf16[3,256,1152]{2,1,0:T(8,128)(2,1)S(1)} %get-tuple-element.60.mine, bf16[3,256,1152]{2,1,0:T(8,128)(2,1)S(1)} %collective-permute-done.7.theirs, bf16[256,512]{1,0:T(8,128)(2,1)S(1)} %get-tuple-element.98.cot_mine, ...), custom_call_target="tpu_custom_call" | custom-call | flops 1811939328 | bytes 7602176 | tf_op jit(solution)/shard_map/pallas_call | solution.py:49
  16.6 0.9 collective-permute-start.16
  17.6 1.7 %collective-permute-done.10.got = bf16[576,256]{1,0:T(8,128)(2,1)S(1)} collective-permute-done((bf16[576,256]{1,0:T(8,128)(2,1)S(1)}, bf16[576,256]{1,0:T(8,128)(2,1)S(1)}, u32[]{:S(2)}, u32[]{:S(2)}) %collective-permute-start.10) | collective-permute-done | bytes 294944 | tf_op jit(solution)/shard_map/ppermute | solution.py:21
  19.3 1.3 %collective-permute-done.8.low = bf16[576,256]{1,0:T(8,128)(2,1)S(1)} collective-permute-done((bf16[576,256]{1,0:T(8,128)(2,1)S(1)}, bf16[576,256]{1,0:T(8,128)(2,1)S(1)}, u32[]{:S(2)}, u32[]{:S(2)}) %collective-permute-start.8) | collective-permute-done | bytes 294944 | tf_op jit(solution)/shard_map/ppermute | solution.py:21
  20.5 0.1 shard_map.97
  20.7 0.7 collective-permute-start.14
  21.4 2.0 %collective-permute-start.15 = (bf16[1440,256]{1,0:T(8,128)(2,1)S(1)}, bf16[1440,256]{1,0:T(8,128)(2,1)S(1)}, u32[]{:S(2)}, u32[]{:S(2)}) collective-permute-start(bf16[1440,256]{1,0:T(8,128)(2,1)S(1)} %get-tuple-element.66), channel_id=1, source_target_pairs={{0,12},{1,13},{2,14},{3,15},{4,0},{5,1},{6,2},{7,3},{8,4},{9,5},{1... | collective-permute-start | bytes 2211848 | tf_op jit(solution)/shard_map/ppermute | solution.py:21
  23.5 1.6 %collective-permute-start.6 = (bf16[288,512]{1,0:T(8,128)(2,1)S(1)}, bf16[288,512]{1,0:T(8,128)(2,1)S(1)}, u32[]{:S(2)}, u32[]{:S(2)}) collective-permute-start(bf16[288,512]{1,0:T(8,128)(2,1)S(1)} %get-tuple-element.56), channel_id=1, source_target_pairs={{0,1},{1,0},{2,3},{3,2},{4,5},{5,4},{6,7},{7,6},{8,9},{9,8},{10,11... | collective-permute-start | bytes 884744 | tf_op jit(solution)/shard_map/ppermute | solution.py:21
  25.1 1.2 %collective-permute-done.6.theirs = bf16[288,512]{1,0:T(8,128)(2,1)S(1)} collective-permute-done((bf16[288,512]{1,0:T(8,128)(2,1)S(1)}, bf16[288,512]{1,0:T(8,128)(2,1)S(1)}, u32[]{:S(2)}, u32[]{:S(2)}) %collective-permute-start.6) | collective-permute-done | bytes 294944 | tf_op jit(solution)/shard_map/ppermute | solution.py:21
  26.4 1.4 %collective-permute-start.11 = (bf16[576,256]{1,0:T(8,128)(2,1)S(1)}, bf16[576,256]{1,0:T(8,128)(2,1)S(1)}, u32[]{:S(2)}, u32[]{:S(2)}) collective-permute-start(bf16[576,256]{1,0:T(8,128)(2,1)S(1)} %get-tuple-element.67.block_b), channel_id=1, source_target_pairs={{0,2},{1,3},{2,0},{3,1},{4,6},{5,7},{6,4},{7,5},{8,10},{9,11},{10,... | collective-permute-start | bytes 884744 | tf_op jit(solution)/shard_map/ppermute | solution.py:21
  27.8 1.7 %collective-permute-start.12 = (bf16[576,256]{1,0:T(8,128)(2,1)S(1)}, bf16[576,256]{1,0:T(8,128)(2,1)S(1)}, u32[]{:S(2)}, u32[]{:S(2)}) collective-permute-start(bf16[576,256]{1,0:T(8,128)(2,1)S(1)} %get-tuple-element.68.block_a), channel_id=1, source_target_pairs={{0,12},{1,13},{2,14},{3,15},{4,0},{5,1},{6,2},{7,3},{8,4},{9,5},{1... | collective-permute-start | bytes 884744 | tf_op jit(solution)/shard_map/ppermute | solution.py:21
  29.4 9.6 %collective-permute-done.14.below = bf16[1440,256]{1,0:T(8,128)(2,1)S(1)} collective-permute-done((bf16[1440,256]{1,0:T(8,128)(2,1)S(1)}, bf16[1440,256]{1,0:T(8,128)(2,1)S(1)}, u32[]{:S(2)}, u32[]{:S(2)}) %collective-permute-start.14) | collective-permute-done | bytes 737312 | tf_op jit(solution)/shard_map/ppermute | solution.py:21
  39.0 0.4 shard_map.99
  39.4 0.4 collective-permute-start.17
  39.9 2.6 %collective-permute-start.18 = (bf16[576,256]{1,0:T(8,128)(2,1)S(1)}, bf16[576,256]{1,0:T(8,128)(2,1)S(1)}, u32[]{:S(2)}, u32[]{:S(2)}) collective-permute-start(bf16[576,256]{1,0:T(8,128)(2,1)S(1)} %get-tuple-element.75), channel_id=1, source_target_pairs={{0,12},{1,13},{2,14},{3,15},{4,0},{5,1},{6,2},{7,3},{8,4},{9,5},{1... | collective-permute-start | bytes 884744 | tf_op jit(solution)/shard_map/ppermute | solution.py:21
  42.4 2.3 %collective-permute-done.11.block_z = bf16[576,256]{1,0:T(8,128)(2,1)S(1)} collective-permute-done((bf16[576,256]{1,0:T(8,128)(2,1)S(1)}, bf16[576,256]{1,0:T(8,128)(2,1)S(1)}, u32[]{:S(2)}, u32[]{:S(2)}) %collective-permute-start.11) | collective-permute-done | bytes 294944 | tf_op jit(solution)/shard_map/ppermute | solution.py:21
  44.8 0.8 collective-permute-start.19
  45.6 1.2 %collective-permute-done.13.below = bf16[576,256]{1,0:T(8,128)(2,1)S(1)} collective-permute-done((bf16[576,256]{1,0:T(8,128)(2,1)S(1)}, bf16[576,256]{1,0:T(8,128)(2,1)S(1)}, u32[]{:S(2)}, u32[]{:S(2)}) %collective-permute-start.13) | collective-permute-done | bytes 294944 | tf_op jit(solution)/shard_map/ppermute | solution.py:21
  46.9 1.6 %shard_map.98 = (bf16[1440,256]{1,0:T(8,128)(2,1)}, bf16[1440,256]{1,0:T(8,128)(2,1)}, bf16[3,576,256]{2,1,0:T(8,128)(2,1)}) custom-call(bf16[576,256]{1,0:T(8,128)(2,1)S(1)} %get-tuple-element.68.block_a, bf16[576,256]{1,0:T(8,128)(2,1)S(1)} %get-tuple-element.67.block_b, bf16[576,256]{1,0:T(8,128)(2,1)S(1)} %collective-permute-done.11.block_z, ...), custom_call_target="tpu_custom_call" | custom-call | bytes 3833856 | tf_op jit(solution)/shard_map/pallas_call | solution.py:49
  48.5 4.7 %collective-permute-done.17.below = bf16[576,256]{1,0:T(8,128)(2,1)S(1)} collective-permute-done((bf16[576,256]{1,0:T(8,128)(2,1)S(1)}, bf16[576,256]{1,0:T(8,128)(2,1)S(1)}, u32[]{:S(2)}, u32[]{:S(2)}) %collective-permute-start.17) | collective-permute-done | bytes 294944 | tf_op jit(solution)/shard_map/ppermute | solution.py:21
  53.3 0.7 collective-permute-start.20
  54.0 1.9 %collective-permute-start.21 = (bf16[1440,256]{1,0:T(8,128)(2,1)}, bf16[1440,256]{1,0:T(8,128)(2,1)S(1)}, u32[]{:S(2)}, u32[]{:S(2)}) collective-permute-start(bf16[1440,256]{1,0:T(8,128)(2,1)} %get-tuple-element.78), channel_id=1, source_target_pairs={{0,12},{1,13},{2,14},{3,15},{4,0},{5,1},{6,2},{7,3},{8,4},{9,5},{1... | collective-permute-start | bytes 2211848 | tf_op jit(solution)/shard_map/ppermute | solution.py:21
  56.0 0.2 shard_map.100
  56.2 0.8 copy-done.3
  57.0 4.0 %collective-permute-start.22 = (bf16[288,512]{1,0:T(8,128)(2,1)S(1)}, bf16[288,512]{1,0:T(8,128)(2,1)}, u32[]{:S(2)}, u32[]{:S(2)}) collective-permute-start(bf16[288,512]{1,0:T(8,128)(2,1)S(1)} %get-tuple-element.82), channel_id=1, source_target_pairs={{0,1},{1,0},{2,3},{3,2},{4,5},{5,4},{6,7},{7,6},{8,9},{9,8},{10,11... | collective-permute-start | bytes 884744 | tf_op jit(solution)/shard_map/ppermute | solution.py:21
  61.8 0.7 pad_maximum_fusion.rates
  62.5 5.7 %shard_map.101 = (f32[1,288,1024]{2,1,0:T(8,128)}, f32[1,288,1024]{2,1,0:T(8,128)}, f32[288,1024]{1,0:T(8,128)}, bf16[288,1024]{1,0:T(8,128)(2,1)}) custom-call(f32[2]{0:T(128)} %pad_maximum_fusion.rates, f32[288,512]{1,0:T(8,128)} %copy-done.3, bf16[288,512]{1,0:T(8,128)(2,1)} %collective-permute-done.22.other, f32[1,288,1024]{2,1,0:T(8,128)} %master.1, ...), custom_call_target="tpu_custom_call" | custom-call | flops 5898240 | bytes 8847360 | tf_op jit(solution)/shard_map/pallas_call | solution.py:281
  68.1 24.9 %conditional.1 = (bf16[288,1024]{1,0:T(8,128)(2,1)}) conditional(s32[]{:T(128)} %clamp.3, bf16[288,1024]{1,0:T(8,128)(2,1)} %get-tuple-element.83, bf16[288,1024]{1,0:T(8,128)(2,1)} %get-tuple-element.83, bf16[288,1024]{1,0:T(8,128)(2,1)} %get-tuple-element.83, bf16[288,1024]{1,0:T(8,128)(2,1)} %get-tuple-element.83), branch_computations={%region_0.1_spmd, %region_1.2_spmd, %region_2.3_spmd, %region_3.4_... | conditional | bytes 2359344 | solution.py:376
  68.1 5.0 %collective-permute-start.3 = (bf16[288,1024]{1,0:T(8,128)(2,1)}, bf16[288,1024]{1,0:T(8,128)(2,1)}, u32[]{:S(2)}, u32[]{:S(2)}) collective-permute-start(bf16[288,1024]{1,0:T(8,128)(2,1)} %param.3), channel_id=1, source_target_pairs={{0,128},{16,144},{32,160},{48,176},{64,192},{80,208},{96,224},{112... | collective-permute-start | bytes 1769480 | tf_op jit(solution)/shard_map/cond/branch_3_fun/ppermute | solution.py:27
  73.1 19.9 %collective-permute-done.3 = bf16[288,1024]{1,0:T(8,128)(2,1)} collective-permute-done((bf16[288,1024]{1,0:T(8,128)(2,1)}, bf16[288,1024]{1,0:T(8,128)(2,1)}, u32[]{:S(2)}, u32[]{:S(2)}) %collective-permute-start.3) | collective-permute-done | bytes 589856 | tf_op jit(solution)/shard_map/cond/branch_3_fun/ppermute | solution.py:27
  93.1 8.5 %collective-permute-start.23 = (bf16[576,256]{1,0:T(8,128)(2,1)S(1)}, bf16[576,256]{1,0:T(8,128)(2,1)S(1)}, u32[]{:S(2)}, u32[]{:S(2)}) collective-permute-start(bf16[576,256]{1,0:T(8,128)(2,1)S(1)} %get-tuple-element.86.line), channel_id=1, source_target_pairs={{0,2},{1,3},{2,0},{3,1},{4,6},{5,7},{6,4},{7,5},{8,10},{9,11},{10,... | collective-permute-start | bytes 884744 | tf_op jit(solution)/shard_map/ppermute | solution.py:21
  101.6 2.7 %collective-permute-start.25 = (bf16[576,256]{1,0:T(8,128)(2,1)S(1)}, bf16[576,256]{1,0:T(8,128)(2,1)S(1)}, u32[]{:S(2)}, u32[]{:S(2)}) collective-permute-start(bf16[576,256]{1,0:T(8,128)(2,1)S(1)} %get-tuple-element.88), channel_id=1, source_target_pairs={{0,12},{1,13},{2,14},{3,15},{4,0},{5,1},{6,2},{7,3},{8,4},{9,5},{1... | collective-permute-start | bytes 884744 | tf_op jit(solution)/shard_map/ppermute | solution.py:21
  104.3 1.5 %copy-done.2 = bf16[3,256,1152]{2,1,0:T(8,128)(2,1)S(1)} copy-done((bf16[3,256,1152]{2,1,0:T(8,128)(2,1)S(1)}, bf16[3,256,1152]{2,1,0:T(8,128)(2,1)}, u32[]{:S(2)}) %copy-start.2) | copy-done | bytes 1769496
  105.8 3.9 %shard_map.103.before = f32[512,512]{1,0:T(8,128)S(1)} custom-call(bf16[3,256,1152]{2,1,0:T(8,128)(2,1)S(1)} %get-tuple-element.60.mine, bf16[3,256,1152]{2,1,0:T(8,128)(2,1)S(1)} %copy-done.2, bf16[3,576,256]{2,1,0:T(8,128)(2,1)} %get-tuple-element.89.along, bf16[3,576,256]{2,1,0:T(8,128)(2,1)} %collective-permute-done.26.got_z, ...), custom_call_target="tpu_custom_call" | custom-call | flops 1811939328 | bytes 8568832 | tf_op jit(solution)/shard_map/pallas_call | solution.py:49
  109.8 0.9 shard_map.104
  110.6 4.4 %collective-permute-start.27 = (bf16[256,512]{1,0:T(8,128)(2,1)S(1)}, bf16[256,512]{1,0:T(8,128)(2,1)S(1)}, u32[]{:S(2)}, u32[]{:S(2)}) collective-permute-start(bf16[256,512]{1,0:T(8,128)(2,1)S(1)} %get-tuple-element.91), channel_id=1, source_target_pairs={{0,1},{1,0},{2,3},{3,2},{4,5},{5,4},{6,7},{7,6},{8,9},{9,8},{10,11... | collective-permute-start | bytes 786440 | tf_op jit(solution)/shard_map/ppermute | solution.py:21
  115.1 2.3 %multiply_bitcast_fusion = f32[1,288,1024]{2,1,0:T(8,128)} fusion(f32[288,1024]{1,0:T(8,128)S(1)} %copy-done.9, bf16[288,1024]{1,0:T(8,128)(2,1)} %get-tuple-element.99), kind=kLoop, calls=%fused_computation | loop fusion | flops 884736 | bytes 2949120 | tf_op jit(solution)/shard_map/broadcast_in_dim | solution.py:408
  117.4 0.9 shard_map.105
  (42 shorter events, 0.4 us)
Async XLA Ops:
  0.6 1.7 %copy-start = (bf16[256,4608]{1,0:T(8,128)(2,1)S(1)}, bf16[256,4608]{1,0:T(8,128)(2,1)}, u32[]{:S(2)}) copy-start(bf16[256,4608]{1,0:T(8,128)(2,1)} %tokens.1) | copy-start | bytes 7077892
  2.3 5.3 %copy-start.10 = (bf16[256,1024]{1,0:T(8,128)(2,1)S(1)}, bf16[256,1024]{1,0:T(8,128)(2,1)}, u32[]{:S(2)}) copy-start(bf16[256,1024]{1,0:T(8,128)(2,1)} %param.11) | copy-start | bytes 1572868
  4.2 6.2 %copy-start.4 = (bf16[256,1152]{1,0:T(8,128)(2,1)}, bf16[256,1152]{1,0:T(8,128)(2,1)S(1)}, u32[]{:S(2)}) copy-start(bf16[256,1152]{1,0:T(8,128)(2,1)S(1)} %get-tuple-element.54.mine) | copy-start | bytes 1769476
  4.2 5.3 %collective-permute-start.4 = (bf16[256,1152]{1,0:T(8,128)(2,1)S(1)}, bf16[256,1152]{1,0:T(8,128)(2,1)S(1)}, u32[]{:S(2)}, u32[]{:S(2)}) collective-permute-start(bf16[256,1152]{1,0:T(8,128)(2,1)S(1)} %get-tuple-element.54.mine), channel_id=1, source_target_pairs={{0,1},{1,0},{2,3},{3,2},{4,5},{5,4},{6,7},{7,6},{8,9},{9,8},{10,11... | collective-permute-start | bytes 1769480 | tf_op jit(solution)/shard_map/ppermute | solution.py:21
  7.6 2.0 %collective-permute-start.5 = (bf16[256,512]{1,0:T(8,128)(2,1)S(1)}, bf16[256,512]{1,0:T(8,128)(2,1)S(1)}, u32[]{:S(2)}, u32[]{:S(2)}) collective-permute-start(bf16[256,512]{1,0:T(8,128)(2,1)S(1)} %get-tuple-element.97), channel_id=1, source_target_pairs={{0,1},{1,0},{2,3},{3,2},{4,5},{5,4},{6,7},{7,6},{8,9},{9,8},{10,11... | collective-permute-start | bytes 786440 | tf_op jit(solution)/shard_map/ppermute | solution.py:21
  9.6 7.0 %copy-start.6 = (bf16[256,1152]{1,0:T(8,128)(2,1)}, bf16[256,1152]{1,0:T(8,128)(2,1)S(1)}, u32[]{:S(2)}) copy-start(bf16[256,1152]{1,0:T(8,128)(2,1)S(1)} %collective-permute-done.4.theirs) | copy-start | bytes 1769476
  10.4 3.8 %collective-permute-start.7 = (bf16[3,256,1152]{2,1,0:T(8,128)(2,1)S(1)}, bf16[3,256,1152]{2,1,0:T(8,128)(2,1)S(1)}, u32[]{:S(2)}, u32[]{:S(2)}) collective-permute-start(bf16[3,256,1152]{2,1,0:T(8,128)(2,1)S(1)} %get-tuple-element.60.mine), channel_id=1, source_target_pairs={{0,1},{1,0},{2,3},{3,2},{4,5},{5,4},{6,7},{7,6},{8,9},{9,8},{10,11... | collective-permute-start | bytes 5308424 | tf_op jit(solution)/shard_map/ppermute | solution.py:21
  10.9 9.7 %collective-permute-start.8 = (bf16[576,256]{1,0:T(8,128)(2,1)S(1)}, bf16[576,256]{1,0:T(8,128)(2,1)S(1)}, u32[]{:S(2)}, u32[]{:S(2)}) collective-permute-start(bf16[576,256]{1,0:T(8,128)(2,1)S(1)} %get-tuple-element.55), channel_id=1, source_target_pairs={{0,4},{1,5},{2,6},{3,7},{4,8},{5,9},{6,10},{7,11},{8,12},{9,13},{1... | collective-permute-start | bytes 884744 | tf_op jit(solution)/shard_map/ppermute | solution.py:21
  10.9 8.4 %collective-permute-start.10 = (bf16[576,256]{1,0:T(8,128)(2,1)S(1)}, bf16[576,256]{1,0:T(8,128)(2,1)S(1)}, u32[]{:S(2)}, u32[]{:S(2)}) collective-permute-start(bf16[576,256]{1,0:T(8,128)(2,1)S(1)} %get-tuple-element.64), channel_id=1, source_target_pairs={{0,2},{1,3},{2,0},{3,1},{4,6},{5,7},{6,4},{7,5},{8,10},{9,11},{10,... | collective-permute-start | bytes 884744 | tf_op jit(solution)/shard_map/ppermute | solution.py:21
  12.1 8.5 %collective-permute-start.9 = (bf16[576,256]{1,0:T(8,128)(2,1)S(1)}, bf16[576,256]{1,0:T(8,128)(2,1)S(1)}, u32[]{:S(2)}, u32[]{:S(2)}) collective-permute-start(bf16[576,256]{1,0:T(8,128)(2,1)S(1)} %get-tuple-element.62), channel_id=1, source_target_pairs={{0,12},{1,13},{2,14},{3,15},{4,0},{5,1},{6,2},{7,3},{8,4},{9,5},{1... | collective-permute-start | bytes 884744 | tf_op jit(solution)/shard_map/ppermute | solution.py:21
  14.2 2.4 %copy-start.1 = (bf16[3,256,1152]{2,1,0:T(8,128)(2,1)}, bf16[3,256,1152]{2,1,0:T(8,128)(2,1)S(1)}, u32[]{:S(2)}) copy-start(bf16[3,256,1152]{2,1,0:T(8,128)(2,1)S(1)} %collective-permute-done.7.theirs) | copy-start | bytes 5308420
  16.6 22.4 %collective-permute-start.16 = (bf16[3,576,256]{2,1,0:T(8,128)(2,1)S(1)}, bf16[3,576,256]{2,1,0:T(8,128)(2,1)S(1)}, u32[]{:S(2)}, u32[]{:S(2)}) collective-permute-start(bf16[3,576,256]{2,1,0:T(8,128)(2,1)S(1)} %get-tuple-element.73), channel_id=1, source_target_pairs={{0,2},{1,3},{2,0},{3,1},{4,6},{5,7},{6,4},{7,5},{8,10},{9,11},{10,... | collective-permute-start | bytes 2654216 | tf_op jit(solution)/shard_map/ppermute | solution.py:21
  20.5 2.9 %copy-start.8 = (f32[1,288,1024]{2,1,0:T(8,128)S(1)}, f32[1,288,1024]{2,1,0:T(8,128)}, u32[]{:S(2)}) copy-start(f32[1,288,1024]{2,1,0:T(8,128)} %master.1) | copy-start | bytes 3538948
  20.7 18.3 %collective-permute-start.14 = (bf16[1440,256]{1,0:T(8,128)(2,1)S(1)}, bf16[1440,256]{1,0:T(8,128)(2,1)S(1)}, u32[]{:S(2)}, u32[]{:S(2)}) collective-permute-start(bf16[1440,256]{1,0:T(8,128)(2,1)S(1)} %get-tuple-element.65), channel_id=1, source_target_pairs={{0,4},{1,5},{2,6},{3,7},{4,8},{5,9},{6,10},{7,11},{8,12},{9,13},{1... | collective-permute-start | bytes 2211848 | tf_op jit(solution)/shard_map/ppermute | solution.py:21
  21.4 17.6 %collective-permute-start.15 = (bf16[1440,256]{1,0:T(8,128)(2,1)S(1)}, bf16[1440,256]{1,0:T(8,128)(2,1)S(1)}, u32[]{:S(2)}, u32[]{:S(2)}) collective-permute-start(bf16[1440,256]{1,0:T(8,128)(2,1)S(1)} %get-tuple-element.66), channel_id=1, source_target_pairs={{0,12},{1,13},{2,14},{3,15},{4,0},{5,1},{6,2},{7,3},{8,4},{9,5},{1... | collective-permute-start | bytes 2211848 | tf_op jit(solution)/shard_map/ppermute | solution.py:21
  23.5 2.8 %collective-permute-start.6 = (bf16[288,512]{1,0:T(8,128)(2,1)S(1)}, bf16[288,512]{1,0:T(8,128)(2,1)S(1)}, u32[]{:S(2)}, u32[]{:S(2)}) collective-permute-start(bf16[288,512]{1,0:T(8,128)(2,1)S(1)} %get-tuple-element.56), channel_id=1, source_target_pairs={{0,1},{1,0},{2,3},{3,2},{4,5},{5,4},{6,7},{7,6},{8,9},{9,8},{10,11... | collective-permute-start | bytes 884744 | tf_op jit(solution)/shard_map/ppermute | solution.py:21
  26.4 18.4 %collective-permute-start.11 = (bf16[576,256]{1,0:T(8,128)(2,1)S(1)}, bf16[576,256]{1,0:T(8,128)(2,1)S(1)}, u32[]{:S(2)}, u32[]{:S(2)}) collective-permute-start(bf16[576,256]{1,0:T(8,128)(2,1)S(1)} %get-tuple-element.67.block_b), channel_id=1, source_target_pairs={{0,2},{1,3},{2,0},{3,1},{4,6},{5,7},{6,4},{7,5},{8,10},{9,11},{10,... | collective-permute-start | bytes 884744 | tf_op jit(solution)/shard_map/ppermute | solution.py:21
  27.8 17.9 %collective-permute-start.12 = (bf16[576,256]{1,0:T(8,128)(2,1)S(1)}, bf16[576,256]{1,0:T(8,128)(2,1)S(1)}, u32[]{:S(2)}, u32[]{:S(2)}) collective-permute-start(bf16[576,256]{1,0:T(8,128)(2,1)S(1)} %get-tuple-element.68.block_a), channel_id=1, source_target_pairs={{0,12},{1,13},{2,14},{3,15},{4,0},{5,1},{6,2},{7,3},{8,4},{9,5},{1... | collective-permute-start | bytes 884744 | tf_op jit(solution)/shard_map/ppermute | solution.py:21
  39.0 7.8 %collective-permute-start.13 = (bf16[576,256]{1,0:T(8,128)(2,1)S(1)}, bf16[576,256]{1,0:T(8,128)(2,1)S(1)}, u32[]{:S(2)}, u32[]{:S(2)}) collective-permute-start(bf16[576,256]{1,0:T(8,128)(2,1)S(1)} %get-tuple-element.68.block_a), channel_id=1, source_target_pairs={{0,4},{1,5},{2,6},{3,7},{4,8},{5,9},{6,10},{7,11},{8,12},{9,13},{1... | collective-permute-start | bytes 884744 | tf_op jit(solution)/shard_map/ppermute | solution.py:21
  39.4 13.8 %collective-permute-start.17 = (bf16[576,256]{1,0:T(8,128)(2,1)S(1)}, bf16[576,256]{1,0:T(8,128)(2,1)S(1)}, u32[]{:S(2)}, u32[]{:S(2)}) collective-permute-start(bf16[576,256]{1,0:T(8,128)(2,1)S(1)} %get-tuple-element.74), channel_id=1, source_target_pairs={{0,4},{1,5},{2,6},{3,7},{4,8},{5,9},{6,10},{7,11},{8,12},{9,13},{1... | collective-permute-start | bytes 884744 | tf_op jit(solution)/shard_map/ppermute | solution.py:21
  39.9 13.3 %collective-permute-start.18 = (bf16[576,256]{1,0:T(8,128)(2,1)S(1)}, bf16[576,256]{1,0:T(8,128)(2,1)S(1)}, u32[]{:S(2)}, u32[]{:S(2)}) collective-permute-start(bf16[576,256]{1,0:T(8,128)(2,1)S(1)} %get-tuple-element.75), channel_id=1, source_target_pairs={{0,12},{1,13},{2,14},{3,15},{4,0},{5,1},{6,2},{7,3},{8,4},{9,5},{1... | collective-permute-start | bytes 884744 | tf_op jit(solution)/shard_map/ppermute | solution.py:21
  44.8 8.4 %collective-permute-start.19 = (bf16[576,256]{1,0:T(8,128)(2,1)S(1)}, bf16[576,256]{1,0:T(8,128)(2,1)S(1)}, u32[]{:S(2)}, u32[]{:S(2)}) collective-permute-start(bf16[576,256]{1,0:T(8,128)(2,1)S(1)} %get-tuple-element.76), channel_id=1, source_target_pairs={{0,2},{1,3},{2,0},{3,1},{4,6},{5,7},{6,4},{7,5},{8,10},{9,11},{10,... | collective-permute-start | bytes 884744 | tf_op jit(solution)/shard_map/ppermute | solution.py:21
  53.2 51.1 %collective-permute-start.26 = (bf16[3,576,256]{2,1,0:T(8,128)(2,1)}, bf16[3,576,256]{2,1,0:T(8,128)(2,1)}, u32[]{:S(2)}, u32[]{:S(2)}) collective-permute-start(bf16[3,576,256]{2,1,0:T(8,128)(2,1)} %get-tuple-element.89.along), channel_id=1, source_target_pairs={{0,2},{1,3},{2,0},{3,1},{4,6},{5,7},{6,4},{7,5},{8,10},{9,11},{10,... | collective-permute-start | bytes 2654216 | tf_op jit(solution)/shard_map/ppermute | solution.py:21
  53.3 39.7 %collective-permute-start.20 = (bf16[1440,256]{1,0:T(8,128)(2,1)}, bf16[1440,256]{1,0:T(8,128)(2,1)S(1)}, u32[]{:S(2)}, u32[]{:S(2)}) collective-permute-start(bf16[1440,256]{1,0:T(8,128)(2,1)} %get-tuple-element.77.own_up), channel_id=1, source_target_pairs={{0,4},{1,5},{2,6},{3,7},{4,8},{5,9},{6,10},{7,11},{8,12},{9,13},{1... | collective-permute-start | bytes 2211848 | tf_op jit(solution)/shard_map/ppermute | solution.py:21
  54.0 39.0 %collective-permute-start.21 = (bf16[1440,256]{1,0:T(8,128)(2,1)}, bf16[1440,256]{1,0:T(8,128)(2,1)S(1)}, u32[]{:S(2)}, u32[]{:S(2)}) collective-permute-start(bf16[1440,256]{1,0:T(8,128)(2,1)} %get-tuple-element.78), channel_id=1, source_target_pairs={{0,12},{1,13},{2,14},{3,15},{4,0},{5,1},{6,2},{7,3},{8,4},{9,5},{1... | collective-permute-start | bytes 2211848 | tf_op jit(solution)/shard_map/ppermute | solution.py:21
  56.1 0.8 copy-start.3
  57.0 5.5 %collective-permute-start.22 = (bf16[288,512]{1,0:T(8,128)(2,1)S(1)}, bf16[288,512]{1,0:T(8,128)(2,1)}, u32[]{:S(2)}, u32[]{:S(2)}) collective-permute-start(bf16[288,512]{1,0:T(8,128)(2,1)S(1)} %get-tuple-element.82), channel_id=1, source_target_pairs={{0,1},{1,0},{2,3},{3,2},{4,5},{5,4},{6,7},{7,6},{8,9},{9,8},{10,11... | collective-permute-start | bytes 884744 | tf_op jit(solution)/shard_map/ppermute | solution.py:21
  68.1 24.9 %collective-permute-start.3 = (bf16[288,1024]{1,0:T(8,128)(2,1)}, bf16[288,1024]{1,0:T(8,128)(2,1)}, u32[]{:S(2)}, u32[]{:S(2)}) collective-permute-start(bf16[288,1024]{1,0:T(8,128)(2,1)} %param.3), channel_id=1, source_target_pairs={{0,128},{16,144},{32,160},{48,176},{64,192},{80,208},{96,224},{112... | collective-permute-start | bytes 1769480 | tf_op jit(solution)/shard_map/cond/branch_3_fun/ppermute | solution.py:27
  93.1 16.7 %collective-permute-start.23 = (bf16[576,256]{1,0:T(8,128)(2,1)S(1)}, bf16[576,256]{1,0:T(8,128)(2,1)S(1)}, u32[]{:S(2)}, u32[]{:S(2)}) collective-permute-start(bf16[576,256]{1,0:T(8,128)(2,1)S(1)} %get-tuple-element.86.line), channel_id=1, source_target_pairs={{0,2},{1,3},{2,0},{3,1},{4,6},{5,7},{6,4},{7,5},{8,10},{9,11},{10,... | collective-permute-start | bytes 884744 | tf_op jit(solution)/shard_map/ppermute | solution.py:21
  101.6 8.1 %collective-permute-start.24 = (bf16[576,256]{1,0:T(8,128)(2,1)S(1)}, bf16[576,256]{1,0:T(8,128)(2,1)S(1)}, u32[]{:S(2)}, u32[]{:S(2)}) collective-permute-start(bf16[576,256]{1,0:T(8,128)(2,1)S(1)} %get-tuple-element.87), channel_id=1, source_target_pairs={{0,4},{1,5},{2,6},{3,7},{4,8},{5,9},{6,10},{7,11},{8,12},{9,13},{1... | collective-permute-start | bytes 884744 | tf_op jit(solution)/shard_map/ppermute | solution.py:21
  101.6 8.1 %collective-permute-start.25 = (bf16[576,256]{1,0:T(8,128)(2,1)S(1)}, bf16[576,256]{1,0:T(8,128)(2,1)S(1)}, u32[]{:S(2)}, u32[]{:S(2)}) collective-permute-start(bf16[576,256]{1,0:T(8,128)(2,1)S(1)} %get-tuple-element.88), channel_id=1, source_target_pairs={{0,12},{1,13},{2,14},{3,15},{4,0},{5,1},{6,2},{7,3},{8,4},{9,5},{1... | collective-permute-start | bytes 884744 | tf_op jit(solution)/shard_map/ppermute | solution.py:21
  104.3 1.5 %copy-start.2 = (bf16[3,256,1152]{2,1,0:T(8,128)(2,1)S(1)}, bf16[3,256,1152]{2,1,0:T(8,128)(2,1)}, u32[]{:S(2)}) copy-start(bf16[3,256,1152]{2,1,0:T(8,128)(2,1)} %copy-done.1) | copy-start | bytes 5308420
  105.8 4.0 %copy-start.5 = (bf16[256,1152]{1,0:T(8,128)(2,1)S(1)}, bf16[256,1152]{1,0:T(8,128)(2,1)}, u32[]{:S(2)}) copy-start(bf16[256,1152]{1,0:T(8,128)(2,1)} %copy-done.4) | copy-start | bytes 1769476
  105.8 4.0 %copy-start.7 = (bf16[256,1152]{1,0:T(8,128)(2,1)S(1)}, bf16[256,1152]{1,0:T(8,128)(2,1)}, u32[]{:S(2)}) copy-start(bf16[256,1152]{1,0:T(8,128)(2,1)} %copy-done.6) | copy-start | bytes 1769476
  109.7 5.3 %copy-start.9 = (f32[288,1024]{1,0:T(8,128)S(1)}, f32[288,1024]{1,0:T(8,128)}, u32[]{:S(2)}) copy-start(f32[288,1024]{1,0:T(8,128)} %get-tuple-element.92) | copy-start | bytes 3538948
  110.6 6.7 %collective-permute-start.27 = (bf16[256,512]{1,0:T(8,128)(2,1)S(1)}, bf16[256,512]{1,0:T(8,128)(2,1)S(1)}, u32[]{:S(2)}, u32[]{:S(2)}) collective-permute-start(bf16[256,512]{1,0:T(8,128)(2,1)S(1)} %get-tuple-element.91), channel_id=1, source_target_pairs={{0,1},{1,0},{2,3},{3,2},{4,5},{5,4},{6,7},{7,6},{8,9},{9,8},{10,11... | collective-permute-start | bytes 786440 | tf_op jit(solution)/shard_map/ppermute | solution.py:21
where the time goes:
time: 119 us; the launch traced here: 118 us
  starting transfers between devices  46.1 us (39%)
  waiting for transfers between devices  44.5 us (37%)
  Pallas kernels  18.9 us (16%)
  local copies, waits for them, and re-layouts  4.1 us (3%)
  other arithmetic  2.95 us (2%)
  between operations  1.66 us (1%)
    ppermute x24, starting transfers between devices, hop(): return lax.ppermute(value, 'fsdp', pairs)  41.1 us
    ppermute x24, waiting for transfers between devices, hop(): return lax.ppermute(value, 'fsdp', pairs)  24.6 us
    ppermute x1, waiting for transfers between devices, gossip(): return lax.ppermute(value, 'peer', pairs)  19.9 us
    pallas_call x11, Pallas kernels, kernel_call(): pl.pallas_call(kernel, in_specs=[pl.BlockSpec(memory_space=pltpu.VMEM)] *...  11.3 us
    pallas_call x1, Pallas kernels, adam(): pl.pallas_call(adam_kernel, grid=(3,), in_specs=[scalar, part, part, full...  5.66 us
    ppermute x1, starting transfers between devices, gossip(): return lax.ppermute(value, 'peer', pairs)  5 us
    unnamed x22, local copies, waits for them, and re-layouts  3.99 us
  transfers between devices with their start and end apart: 25, of which 10 were waited for; matrix products, arithmetic and copies ran while one was open for 3% of the time, Pallas kernels for 12%

commit v1 on v0

--- a/solution.py
+++ b/solution.py
@@ -179,10 +179,10 @@
     block_a[rows:], block_b[rows:] = second[:, :quarter], second[:, quarter:]
 
 
-def gather_2_kernel(block_a, block_b, block_z, above, below, up, down, along):
+def gather_2_kernel(block_a, block_b, block_z, above, below, up, down, along, pair):
     (_, z, _), tall = where(), block_a.shape[0]
     wide, mid = 2 * tall, tall // 2
-    for out in (up, down):
+    for out in (up, down, pair):
         out[:tall] = pick(z, block_b[...], block_z[...])
         out[tall:wide] = pick(z, block_z[...], block_b[...])
     up[wide:] = below[:mid]
@@ -192,11 +192,9 @@
     along[2] = block_a[...]
 
 
-def gather_3_kernel(got_up, got_down, up, down, line):
+def gather_3_kernel(got_up, got_down, line):
     tall = line.shape[0]
     wide, mid = 2 * tall, tall // 2
-    up[...] = got_up[:tall]
-    down[...] = got_down[tall:wide]
     line[:mid] = got_up[wide:]
     line[mid:] = got_down[wide:]
 
@@ -223,13 +221,12 @@
         project(mine[k], theirs[k], whole[...], total)
 
 
-def project_2_kernel(mine, theirs, line, got_z, low, high, before, own, other, whole, total):
+def project_2_kernel(mine, theirs, line, got_z, pair, before, own, other, whole, total):
     _, z, _ = where()
     tall, quarter = line.shape
     count = own.shape[0]
     order_z(z, line[...], got_z[...], whole)
-    whole[:tall, quarter:] = low[...]
-    whole[tall:, quarter:] = high[...]
+    whole[:, quarter:] = pair[...]
     total[...] = before[...]
     project(mine[...], theirs[...], whole[...], total)
     own[...] = (total[:count] * D ** (-0.5)).astype(BF)
@@ -364,22 +361,20 @@
     )
     other = hop(other, dc=1)
 
-    up, down, along = kernel_call(
-        gather_2_kernel, (block_a, block_b, block_z, above, below), (long, long, three)
+    up, down, along, pair = kernel_call(
+        gather_2_kernel, (block_a, block_b, block_z, above, below), (long, long, three, shape(BF, wide, quarter))
     )
     up, down, along = after((up, down, along), last_below, last_above, last_z)
     got_up = hop(up, dy=1)
     got_down = hop(down, dy=-1)
     got_z = hop(along, dz=1)
     new_first, new_second, updated, wire = adam(step, own, other, weight, first_moment, second_moment)
+    (pair,) = after((pair,), other)
+    pair = hop(pair, dy=2)
     levels = lax.axis_size("peer").bit_length() - 1
     partner = lax.switch(step[0] % levels, [partial(gossip, bit=which) for which in range(levels)], wire)
     got_up, got_down = after((got_up, got_down), partner)
-    last_up, last_down, line = kernel_call(
-        gather_3_kernel, (got_up, got_down), (block, block, block), limit=8
-    )
-    last_up = hop(last_up, dy=1)
-    last_down = hop(last_down, dy=-1)
+    (line,) = kernel_call(gather_3_kernel, (got_up, got_down), (block,), limit=8)
     line_z = hop(line, dz=1)
 
     whole = pltpu.VMEM((wide, half), BF)
@@ -394,7 +389,7 @@
     result = shape(BF, tokens_here, half)
     result_own, result_other = kernel_call(
         project_2_kernel,
-        (norm_2, far_2, line, line_z, last_up, last_down, total),
+        (norm_2, far_2, line, line_z, pair, total),
         (result, result),
         (whole, pltpu.VMEM((2 * tokens_here, half), F32)),
         limit=16,

time: 119 us -> 99.2 us (0.83)
  starting transfers between devices: 46.1 us -> 31.1 us
  waiting for transfers between devices: 44.5 us -> 40.3 us
  local copies, waits for them, and re-layouts: 4.1 us -> 2.81 us
    ppermute x24 -> x23, starting transfers between devices: 41.1 us -> 30 us  [hop(): return lax.ppermute(value, 'fsdp', pairs)]
    ppermute x1, waiting for transfers between devices: 19.9 us -> 13.5 us  [gossip(): return lax.ppermute(value, 'peer', pairs)]
    ppermute x1, starting transfers between devices: 5 us -> 1.15 us  [gossip(): return lax.ppermute(value, 'peer', pairs)]
    ppermute x24 -> x23, waiting for transfers between devices: 24.6 us -> 26.8 us  [hop(): return lax.ppermute(value, 'fsdp', pairs)]
    unnamed x22 -> x24, local copies, waits for them, and re-layouts: 3.99 us -> 2.7 us
  transfers between devices with their start and end apart: 25 -> 24, of which waited for: 10 -> 12; matrix products, arithmetic and copies ran while one was open for 3% -> 3% of each run, Pallas kernels for 12% -> 15%
where the time goes in v1:
time: 99.2 us; the launch traced here: 98.8 us
  waiting for transfers between devices  40.3 us (41%)
  starting transfers between devices  31.1 us (31%)
  Pallas kernels  20 us (20%)
  other arithmetic  2.93 us (3%)
  local copies, waits for them, and re-layouts  2.81 us (3%)
  between operations  1.65 us (2%)
    ppermute x23, starting transfers between devices, hop(): return lax.ppermute(value, 'fsdp', pairs)  30 us
    ppermute x23, waiting for transfers between devices, hop(): return lax.ppermute(value, 'fsdp', pairs)  26.8 us
    ppermute x1, waiting for transfers between devices, gossip(): return lax.ppermute(value, 'peer', pairs)  13.5 us
    pallas_call x11, Pallas kernels, kernel_call(): pl.pallas_call(kernel, in_specs=[pl.BlockSpec(memory_space=pltpu.VMEM)] *...  12.4 us
    pallas_call x1, Pallas kernels, adam(): pl.pallas_call(adam_kernel, grid=(3,), in_specs=[scalar, part, part, full...  5.68 us
    unnamed x24, local copies, waits for them, and re-layouts  2.7 us
    broadcast_in_dim x1, other arithmetic, on_device(): return (values, averaged[None], new_first, new_second)  2.3 us
  transfers between devices with their start and end apart: 24, of which 12 were waited for; matrix products, arithmetic and copies ran while one was open for 3% of the time, Pallas kernels for 15%

profile of v1, /device:TPU:1, one launch (start us, length us, event | category | flops | bytes accessed | tf_op | source)
XLA Modules:
  0.0 98.8 jit_solution(8704649242492260137)
XLA Ops:
  0.6 1.7 %copy-done = bf16[256,4608]{1,0:T(8,128)(2,1)S(1)} copy-done((bf16[256,4608]{1,0:T(8,128)(2,1)S(1)}, bf16[256,4608]{1,0:T(8,128)(2,1)}, u32[]{:S(2)}) %copy-start) | copy-done | bytes 2359320
  2.3 1.9 %shard_map.93 = (bf16[256,1152]{1,0:T(8,128)(2,1)S(1)}, bf16[3,256,1152]{2,1,0:T(8,128)(2,1)S(1)}) custom-call(bf16[256,4608]{1,0:T(8,128)(2,1)S(1)} %copy-done), custom_call_target="tpu_custom_call" | custom-call | bytes 4718592 | tf_op jit(solution)/shard_map/pallas_call | solution.py:97
  4.2 3.3 %collective-permute-start.4 = (bf16[256,1152]{1,0:T(8,128)(2,1)S(1)}, bf16[256,1152]{1,0:T(8,128)(2,1)S(1)}, u32[]{:S(2)}, u32[]{:S(2)}) collective-permute-start(bf16[256,1152]{1,0:T(8,128)(2,1)S(1)} %get-tuple-element.53.mine), channel_id=1, source_target_pairs={{0,1},{1,0},{2,3},{3,2},{4,5},{5,4},{6,7},{7,6},{8,9},{9,8},{10,11... | collective-permute-start | bytes 1769480 | tf_op jit(solution)/shard_map/ppermute | solution.py:21
  7.6 0.1 collective-permute-start.5
  7.8 1.8 %collective-permute-done.5.cot_theirs = bf16[256,512]{1,0:T(8,128)(2,1)S(1)} collective-permute-done((bf16[256,512]{1,0:T(8,128)(2,1)S(1)}, bf16[256,512]{1,0:T(8,128)(2,1)S(1)}, u32[]{:S(2)}, u32[]{:S(2)}) %collective-permute-start.5) | collective-permute-done | bytes 262176 | tf_op jit(solution)/shard_map/ppermute | solution.py:21
  9.6 0.8 shard_map.94
  10.4 0.5 collective-permute-start.7
  10.9 1.2 %collective-permute-start.10 = (bf16[576,256]{1,0:T(8,128)(2,1)S(1)}, bf16[576,256]{1,0:T(8,128)(2,1)S(1)}, u32[]{:S(2)}, u32[]{:S(2)}) collective-permute-start(bf16[576,256]{1,0:T(8,128)(2,1)S(1)} %get-tuple-element.63), channel_id=1, source_target_pairs={{0,2},{1,3},{2,0},{3,1},{4,6},{5,7},{6,4},{7,5},{8,10},{9,11},{10,... | collective-permute-start | bytes 884744 | tf_op jit(solution)/shard_map/ppermute | solution.py:21
  12.1 1.5 %collective-permute-start.9 = (bf16[576,256]{1,0:T(8,128)(2,1)S(1)}, bf16[576,256]{1,0:T(8,128)(2,1)S(1)}, u32[]{:S(2)}, u32[]{:S(2)}) collective-permute-start(bf16[576,256]{1,0:T(8,128)(2,1)S(1)} %get-tuple-element.61), channel_id=1, source_target_pairs={{0,12},{1,13},{2,14},{3,15},{4,0},{5,1},{6,2},{7,3},{8,4},{9,5},{1... | collective-permute-start | bytes 884744 | tf_op jit(solution)/shard_map/ppermute | solution.py:21
  13.5 0.6 collective-permute-done.7.theirs
  14.2 2.4 %shard_map.96 = (bf16[3,1152,256]{2,1,0:T(8,128)(2,1)S(1)}, bf16[3,576,256]{2,1,0:T(8,128)(2,1)S(1)}, bf16[3,576,256]{2,1,0:T(8,128)(2,1)S(1)}) custom-call(bf16[3,256,1152]{2,1,0:T(8,128)(2,1)S(1)} %get-tuple-element.59.mine, bf16[3,256,1152]{2,1,0:T(8,128)(2,1)S(1)} %collective-permute-done.7.theirs, bf16[256,512]{1,0:T(8,128)(2,1)S(1)} %get-tuple-element.96.cot_mine, ...), custom_call_target="tpu_custom_call" | custom-call | flops 1811939328 | bytes 7602176 | tf_op jit(solution)/shard_map/pallas_call | solution.py:49
  16.6 0.9 collective-permute-start.16
  17.6 1.7 %collective-permute-done.10.got = bf16[576,256]{1,0:T(8,128)(2,1)S(1)} collective-permute-done((bf16[576,256]{1,0:T(8,128)(2,1)S(1)}, bf16[576,256]{1,0:T(8,128)(2,1)S(1)}, u32[]{:S(2)}, u32[]{:S(2)}) %collective-permute-start.10) | collective-permute-done | bytes 294944 | tf_op jit(solution)/shard_map/ppermute | solution.py:21
  19.3 1.3 %collective-permute-done.8.low = bf16[576,256]{1,0:T(8,128)(2,1)S(1)} collective-permute-done((bf16[576,256]{1,0:T(8,128)(2,1)S(1)}, bf16[576,256]{1,0:T(8,128)(2,1)S(1)}, u32[]{:S(2)}, u32[]{:S(2)}) %collective-permute-start.8) | collective-permute-done | bytes 294944 | tf_op jit(solution)/shard_map/ppermute | solution.py:21
  20.5 0.1 shard_map.97
  20.7 0.7 collective-permute-start.14
  21.4 2.0 %collective-permute-start.15 = (bf16[1440,256]{1,0:T(8,128)(2,1)S(1)}, bf16[1440,256]{1,0:T(8,128)(2,1)S(1)}, u32[]{:S(2)}, u32[]{:S(2)}) collective-permute-start(bf16[1440,256]{1,0:T(8,128)(2,1)S(1)} %get-tuple-element.65), channel_id=1, source_target_pairs={{0,12},{1,13},{2,14},{3,15},{4,0},{5,1},{6,2},{7,3},{8,4},{9,5},{1... | collective-permute-start | bytes 2211848 | tf_op jit(solution)/shard_map/ppermute | solution.py:21
  23.5 1.6 %collective-permute-start.6 = (bf16[288,512]{1,0:T(8,128)(2,1)S(1)}, bf16[288,512]{1,0:T(8,128)(2,1)S(1)}, u32[]{:S(2)}, u32[]{:S(2)}) collective-permute-start(bf16[288,512]{1,0:T(8,128)(2,1)S(1)} %get-tuple-element.55), channel_id=1, source_target_pairs={{0,1},{1,0},{2,3},{3,2},{4,5},{5,4},{6,7},{7,6},{8,9},{9,8},{10,11... | collective-permute-start | bytes 884744 | tf_op jit(solution)/shard_map/ppermute | solution.py:21
  25.1 1.2 %collective-permute-done.6.theirs = bf16[288,512]{1,0:T(8,128)(2,1)S(1)} collective-permute-done((bf16[288,512]{1,0:T(8,128)(2,1)S(1)}, bf16[288,512]{1,0:T(8,128)(2,1)S(1)}, u32[]{:S(2)}, u32[]{:S(2)}) %collective-permute-start.6) | collective-permute-done | bytes 294944 | tf_op jit(solution)/shard_map/ppermute | solution.py:21
  26.4 1.4 %collective-permute-start.11 = (bf16[576,256]{1,0:T(8,128)(2,1)S(1)}, bf16[576,256]{1,0:T(8,128)(2,1)S(1)}, u32[]{:S(2)}, u32[]{:S(2)}) collective-permute-start(bf16[576,256]{1,0:T(8,128)(2,1)S(1)} %get-tuple-element.66.block_b), channel_id=1, source_target_pairs={{0,2},{1,3},{2,0},{3,1},{4,6},{5,7},{6,4},{7,5},{8,10},{9,11},{10,... | collective-permute-start | bytes 884744 | tf_op jit(solution)/shard_map/ppermute | solution.py:21
  27.8 1.7 %collective-permute-start.12 = (bf16[576,256]{1,0:T(8,128)(2,1)S(1)}, bf16[576,256]{1,0:T(8,128)(2,1)S(1)}, u32[]{:S(2)}, u32[]{:S(2)}) collective-permute-start(bf16[576,256]{1,0:T(8,128)(2,1)S(1)} %get-tuple-element.67.block_a), channel_id=1, source_target_pairs={{0,12},{1,13},{2,14},{3,15},{4,0},{5,1},{6,2},{7,3},{8,4},{9,5},{1... | collective-permute-start | bytes 884744 | tf_op jit(solution)/shard_map/ppermute | solution.py:21
  29.4 9.6 %collective-permute-done.14.below = bf16[1440,256]{1,0:T(8,128)(2,1)S(1)} collective-permute-done((bf16[1440,256]{1,0:T(8,128)(2,1)S(1)}, bf16[1440,256]{1,0:T(8,128)(2,1)S(1)}, u32[]{:S(2)}, u32[]{:S(2)}) %collective-permute-start.14) | collective-permute-done | bytes 737312 | tf_op jit(solution)/shard_map/ppermute | solution.py:21
  39.0 0.4 shard_map.99
  39.4 0.4 collective-permute-start.17
  39.9 2.6 %collective-permute-start.18 = (bf16[576,256]{1,0:T(8,128)(2,1)S(1)}, bf16[576,256]{1,0:T(8,128)(2,1)S(1)}, u32[]{:S(2)}, u32[]{:S(2)}) collective-permute-start(bf16[576,256]{1,0:T(8,128)(2,1)S(1)} %get-tuple-element.74), channel_id=1, source_target_pairs={{0,12},{1,13},{2,14},{3,15},{4,0},{5,1},{6,2},{7,3},{8,4},{9,5},{1... | collective-permute-start | bytes 884744 | tf_op jit(solution)/shard_map/ppermute | solution.py:21
  42.4 2.3 %collective-permute-done.11.block_z = bf16[576,256]{1,0:T(8,128)(2,1)S(1)} collective-permute-done((bf16[576,256]{1,0:T(8,128)(2,1)S(1)}, bf16[576,256]{1,0:T(8,128)(2,1)S(1)}, u32[]{:S(2)}, u32[]{:S(2)}) %collective-permute-start.11) | collective-permute-done | bytes 294944 | tf_op jit(solution)/shard_map/ppermute | solution.py:21
  44.8 0.8 collective-permute-start.19
  45.6 1.2 %collective-permute-done.13.below = bf16[576,256]{1,0:T(8,128)(2,1)S(1)} collective-permute-done((bf16[576,256]{1,0:T(8,128)(2,1)S(1)}, bf16[576,256]{1,0:T(8,128)(2,1)S(1)}, u32[]{:S(2)}, u32[]{:S(2)}) %collective-permute-start.13) | collective-permute-done | bytes 294944 | tf_op jit(solution)/shard_map/ppermute | solution.py:21
  46.9 1.8 %shard_map.98 = (bf16[1440,256]{1,0:T(8,128)(2,1)}, bf16[1440,256]{1,0:T(8,128)(2,1)}, bf16[3,576,256]{2,1,0:T(8,128)(2,1)}, bf16[1152,256]{1,0:T(8,128)(2,1)}) custom-call(bf16[576,256]{1,0:T(8,128)(2,1)S(1)} %get-tuple-element.67.block_a, bf16[576,256]{1,0:T(8,128)(2,1)S(1)} %get-tuple-element.66.block_b, ...), custom_call_target="tpu_custom_call" | custom-call | bytes 4423680 | tf_op jit(solution)/shard_map/pallas_call | solution.py:49
  48.7 4.5 %collective-permute-done.17.below = bf16[576,256]{1,0:T(8,128)(2,1)S(1)} collective-permute-done((bf16[576,256]{1,0:T(8,128)(2,1)S(1)}, bf16[576,256]{1,0:T(8,128)(2,1)S(1)}, u32[]{:S(2)}, u32[]{:S(2)}) %collective-permute-start.17) | collective-permute-done | bytes 294944 | tf_op jit(solution)/shard_map/ppermute | solution.py:21
  53.3 0.7 collective-permute-start.20
  54.0 1.9 %collective-permute-start.21 = (bf16[1440,256]{1,0:T(8,128)(2,1)}, bf16[1440,256]{1,0:T(8,128)(2,1)S(1)}, u32[]{:S(2)}, u32[]{:S(2)}) collective-permute-start(bf16[1440,256]{1,0:T(8,128)(2,1)} %get-tuple-element.77), channel_id=1, source_target_pairs={{0,12},{1,13},{2,14},{3,15},{4,0},{5,1},{6,2},{7,3},{8,4},{9,5},{1... | collective-permute-start | bytes 2211848 | tf_op jit(solution)/shard_map/ppermute | solution.py:21
  56.0 0.2 shard_map.100
  56.2 0.9 copy-done.3
  57.0 4.0 %collective-permute-start.22 = (bf16[288,512]{1,0:T(8,128)(2,1)S(1)}, bf16[288,512]{1,0:T(8,128)(2,1)S(1)}, u32[]{:S(2)}, u32[]{:S(2)}) collective-permute-start(bf16[288,512]{1,0:T(8,128)(2,1)S(1)} %get-tuple-element.81), channel_id=1, source_target_pairs={{0,1},{1,0},{2,3},{3,2},{4,5},{5,4},{6,7},{7,6},{8,9},{9,8},{10,11... | collective-permute-start | bytes 884744 | tf_op jit(solution)/shard_map/ppermute | solution.py:21
  61.0 1.2 %collective-permute-done.22.other = bf16[288,512]{1,0:T(8,128)(2,1)S(1)} collective-permute-done((bf16[288,512]{1,0:T(8,128)(2,1)S(1)}, bf16[288,512]{1,0:T(8,128)(2,1)S(1)}, u32[]{:S(2)}, u32[]{:S(2)}) %collective-permute-start.22) | collective-permute-done | bytes 294944 | tf_op jit(solution)/shard_map/ppermute | solution.py:21
  63.1 0.6 pad_maximum_fusion.rates
  63.7 5.7 %shard_map.101 = (f32[1,288,1024]{2,1,0:T(8,128)}, f32[1,288,1024]{2,1,0:T(8,128)}, f32[288,1024]{1,0:T(8,128)}, bf16[288,1024]{1,0:T(8,128)(2,1)}) custom-call(f32[2]{0:T(128)} %pad_maximum_fusion.rates, f32[288,512]{1,0:T(8,128)} %copy-done.3, bf16[288,512]{1,0:T(8,128)(2,1)} %copy-done.11, f32[1,288,1024]{2,1,0:T(8,128)} %master.1, ...), custom_call_target="tpu_custom_call" | custom-call | flops 5898240 | bytes 8847360 | tf_op jit(solution)/shard_map/pallas_call | solution.py:278
  69.4 14.7 %conditional.1 = (bf16[288,1024]{1,0:T(8,128)(2,1)}) conditional(s32[]{:T(128)} %clamp.3, bf16[288,1024]{1,0:T(8,128)(2,1)} %get-tuple-element.82, bf16[288,1024]{1,0:T(8,128)(2,1)} %get-tuple-element.82, bf16[288,1024]{1,0:T(8,128)(2,1)} %get-tuple-element.82, bf16[288,1024]{1,0:T(8,128)(2,1)} %get-tuple-element.82), branch_computations={%region_0.1_spmd, %region_1.2_spmd, %region_2.3_spmd, %region_3.4_... | conditional | bytes 2359344 | solution.py:375
  69.4 1.1 %collective-permute-start = (bf16[288,1024]{1,0:T(8,128)(2,1)}, bf16[288,1024]{1,0:T(8,128)(2,1)}, u32[]{:S(2)}, u32[]{:S(2)}) collective-permute-start(bf16[288,1024]{1,0:T(8,128)(2,1)} %param), channel_id=1, source_target_pairs={{0,16},{16,0},{32,48},{48,32},{64,80},{80,64},{96,112},{112,96},{1... | collective-permute-start | bytes 1769480 | tf_op jit(solution)/shard_map/cond/branch_0_fun/ppermute | solution.py:27
  70.6 13.5 %collective-permute-done = bf16[288,1024]{1,0:T(8,128)(2,1)} collective-permute-done((bf16[288,1024]{1,0:T(8,128)(2,1)}, bf16[288,1024]{1,0:T(8,128)(2,1)}, u32[]{:S(2)}, u32[]{:S(2)}) %collective-permute-start) | collective-permute-done | bytes 589856 | tf_op jit(solution)/shard_map/cond/branch_0_fun/ppermute | solution.py:27
  84.2 1.3 %collective-permute-start.23 = (bf16[576,256]{1,0:T(8,128)(2,1)S(1)}, bf16[576,256]{1,0:T(8,128)(2,1)S(1)}, u32[]{:S(2)}, u32[]{:S(2)}) collective-permute-start(bf16[576,256]{1,0:T(8,128)(2,1)S(1)} %shard_map.102.line), channel_id=1, source_target_pairs={{0,2},{1,3},{2,0},{3,1},{4,6},{5,7},{6,4},{7,5},{8,10},{9,11},{10,... | collective-permute-start | bytes 884744 | tf_op jit(solution)/shard_map/ppermute | solution.py:21
  85.6 3.8 %shard_map.103.before = f32[512,512]{1,0:T(8,128)S(1)} custom-call(bf16[3,256,1152]{2,1,0:T(8,128)(2,1)S(1)} %get-tuple-element.59.mine, bf16[3,256,1152]{2,1,0:T(8,128)(2,1)S(1)} %copy-done.2, bf16[3,576,256]{2,1,0:T(8,128)(2,1)} %get-tuple-element.87.along, bf16[3,576,256]{2,1,0:T(8,128)(2,1)} %collective-permute-done.25.got_z, ...), custom_call_target="tpu_custom_call" | custom-call | flops 1811939328 | bytes 8568832 | tf_op jit(solution)/shard_map/pallas_call | solution.py:49
  89.4 1.2 %collective-permute-done.23.got_z = bf16[576,256]{1,0:T(8,128)(2,1)S(1)} collective-permute-done((bf16[576,256]{1,0:T(8,128)(2,1)S(1)}, bf16[576,256]{1,0:T(8,128)(2,1)S(1)}, u32[]{:S(2)}, u32[]{:S(2)}) %collective-permute-start.23) | collective-permute-done | bytes 294944 | tf_op jit(solution)/shard_map/ppermute | solution.py:21
  90.6 1.9 %shard_map.104 = (bf16[256,512]{1,0:T(8,128)(2,1)S(1)}, bf16[256,512]{1,0:T(8,128)(2,1)S(1)}) custom-call(bf16[256,1152]{1,0:T(8,128)(2,1)S(1)} %copy-done.5, bf16[256,1152]{1,0:T(8,128)(2,1)S(1)} %copy-done.7, bf16[576,256]{1,0:T(8,128)(2,1)S(1)} %shard_map.102.line, bf16[576,256]{1,0:T(8,128)(2,1)S(1)} %collective-permute-done.23.got_z, ...), custom_call_target="tpu_custom_call" | custom-call | flops 603979776 | bytes 3932160 | tf_op jit(solution)/shard_map/pallas_call | solution.py:49
  92.5 3.1 %collective-permute-start.26 = (bf16[256,512]{1,0:T(8,128)(2,1)S(1)}, bf16[256,512]{1,0:T(8,128)(2,1)S(1)}, u32[]{:S(2)}, u32[]{:S(2)}) collective-permute-start(bf16[256,512]{1,0:T(8,128)(2,1)S(1)} %get-tuple-element.89), channel_id=1, source_target_pairs={{0,1},{1,0},{2,3},{3,2},{4,5},{5,4},{6,7},{7,6},{8,9},{9,8},{10,11... | collective-permute-start | bytes 786440 | tf_op jit(solution)/shard_map/ppermute | solution.py:21
  95.7 2.3 %multiply_bitcast_fusion = f32[1,288,1024]{2,1,0:T(8,128)} fusion(f32[288,1024]{1,0:T(8,128)S(1)} %copy-done.9, bf16[288,1024]{1,0:T(8,128)(2,1)} %get-tuple-element.97), kind=kLoop, calls=%fused_computation | loop fusion | flops 884736 | bytes 2949120 | tf_op jit(solution)/shard_map/broadcast_in_dim | solution.py:403
  98.0 0.9 shard_map.105
  (42 shorter events, 0.5 us)
Async XLA Ops:
  0.6 1.7 %copy-start = (bf16[256,4608]{1,0:T(8,128)(2,1)S(1)}, bf16[256,4608]{1,0:T(8,128)(2,1)}, u32[]{:S(2)}) copy-start(bf16[256,4608]{1,0:T(8,128)(2,1)} %tokens.1) | copy-start | bytes 7077892
  2.3 5.3 %copy-start.10 = (bf16[256,1024]{1,0:T(8,128)(2,1)S(1)}, bf16[256,1024]{1,0:T(8,128)(2,1)}, u32[]{:S(2)}) copy-start(bf16[256,1024]{1,0:T(8,128)(2,1)} %param.11) | copy-start | bytes 1572868
  4.2 6.2 %copy-start.4 = (bf16[256,1152]{1,0:T(8,128)(2,1)}, bf16[256,1152]{1,0:T(8,128)(2,1)S(1)}, u32[]{:S(2)}) copy-start(bf16[256,1152]{1,0:T(8,128)(2,1)S(1)} %get-tuple-element.53.mine) | copy-start | bytes 1769476
  4.2 5.3 %collective-permute-start.4 = (bf16[256,1152]{1,0:T(8,128)(2,1)S(1)}, bf16[256,1152]{1,0:T(8,128)(2,1)S(1)}, u32[]{:S(2)}, u32[]{:S(2)}) collective-permute-start(bf16[256,1152]{1,0:T(8,128)(2,1)S(1)} %get-tuple-element.53.mine), channel_id=1, source_target_pairs={{0,1},{1,0},{2,3},{3,2},{4,5},{5,4},{6,7},{7,6},{8,9},{9,8},{10,11... | collective-permute-start | bytes 1769480 | tf_op jit(solution)/shard_map/ppermute | solution.py:21
  7.6 2.0 %collective-permute-start.5 = (bf16[256,512]{1,0:T(8,128)(2,1)S(1)}, bf16[256,512]{1,0:T(8,128)(2,1)S(1)}, u32[]{:S(2)}, u32[]{:S(2)}) collective-permute-start(bf16[256,512]{1,0:T(8,128)(2,1)S(1)} %get-tuple-element.95), channel_id=1, source_target_pairs={{0,1},{1,0},{2,3},{3,2},{4,5},{5,4},{6,7},{7,6},{8,9},{9,8},{10,11... | collective-permute-start | bytes 786440 | tf_op jit(solution)/shard_map/ppermute | solution.py:21
  9.6 7.0 %copy-start.6 = (bf16[256,1152]{1,0:T(8,128)(2,1)}, bf16[256,1152]{1,0:T(8,128)(2,1)S(1)}, u32[]{:S(2)}) copy-start(bf16[256,1152]{1,0:T(8,128)(2,1)S(1)} %collective-permute-done.4.theirs) | copy-start | bytes 1769476
  10.4 3.8 %collective-permute-start.7 = (bf16[3,256,1152]{2,1,0:T(8,128)(2,1)S(1)}, bf16[3,256,1152]{2,1,0:T(8,128)(2,1)S(1)}, u32[]{:S(2)}, u32[]{:S(2)}) collective-permute-start(bf16[3,256,1152]{2,1,0:T(8,128)(2,1)S(1)} %get-tuple-element.59.mine), channel_id=1, source_target_pairs={{0,1},{1,0},{2,3},{3,2},{4,5},{5,4},{6,7},{7,6},{8,9},{9,8},{10,11... | collective-permute-start | bytes 5308424 | tf_op jit(solution)/shard_map/ppermute | solution.py:21
  10.9 9.7 %collective-permute-start.8 = (bf16[576,256]{1,0:T(8,128)(2,1)S(1)}, bf16[576,256]{1,0:T(8,128)(2,1)S(1)}, u32[]{:S(2)}, u32[]{:S(2)}) collective-permute-start(bf16[576,256]{1,0:T(8,128)(2,1)S(1)} %get-tuple-element.54), channel_id=1, source_target_pairs={{0,4},{1,5},{2,6},{3,7},{4,8},{5,9},{6,10},{7,11},{8,12},{9,13},{1... | collective-permute-start | bytes 884744 | tf_op jit(solution)/shard_map/ppermute | solution.py:21
  10.9 8.4 %collective-permute-start.10 = (bf16[576,256]{1,0:T(8,128)(2,1)S(1)}, bf16[576,256]{1,0:T(8,128)(2,1)S(1)}, u32[]{:S(2)}, u32[]{:S(2)}) collective-permute-start(bf16[576,256]{1,0:T(8,128)(2,1)S(1)} %get-tuple-element.63), channel_id=1, source_target_pairs={{0,2},{1,3},{2,0},{3,1},{4,6},{5,7},{6,4},{7,5},{8,10},{9,11},{10,... | collective-permute-start | bytes 884744 | tf_op jit(solution)/shard_map/ppermute | solution.py:21
  12.1 8.5 %collective-permute-start.9 = (bf16[576,256]{1,0:T(8,128)(2,1)S(1)}, bf16[576,256]{1,0:T(8,128)(2,1)S(1)}, u32[]{:S(2)}, u32[]{:S(2)}) collective-permute-start(bf16[576,256]{1,0:T(8,128)(2,1)S(1)} %get-tuple-element.61), channel_id=1, source_target_pairs={{0,12},{1,13},{2,14},{3,15},{4,0},{5,1},{6,2},{7,3},{8,4},{9,5},{1... | collective-permute-start | bytes 884744 | tf_op jit(solution)/shard_map/ppermute | solution.py:21
  14.2 2.4 %copy-start.1 = (bf16[3,256,1152]{2,1,0:T(8,128)(2,1)}, bf16[3,256,1152]{2,1,0:T(8,128)(2,1)S(1)}, u32[]{:S(2)}) copy-start(bf16[3,256,1152]{2,1,0:T(8,128)(2,1)S(1)} %collective-permute-done.7.theirs) | copy-start | bytes 5308420
  16.6 22.4 %collective-permute-start.16 = (bf16[3,576,256]{2,1,0:T(8,128)(2,1)S(1)}, bf16[3,576,256]{2,1,0:T(8,128)(2,1)S(1)}, u32[]{:S(2)}, u32[]{:S(2)}) collective-permute-start(bf16[3,576,256]{2,1,0:T(8,128)(2,1)S(1)} %get-tuple-element.72), channel_id=1, source_target_pairs={{0,2},{1,3},{2,0},{3,1},{4,6},{5,7},{6,4},{7,5},{8,10},{9,11},{10,... | collective-permute-start | bytes 2654216 | tf_op jit(solution)/shard_map/ppermute | solution.py:21
  20.5 2.9 %copy-start.8 = (f32[1,288,1024]{2,1,0:T(8,128)S(1)}, f32[1,288,1024]{2,1,0:T(8,128)}, u32[]{:S(2)}) copy-start(f32[1,288,1024]{2,1,0:T(8,128)} %master.1) | copy-start | bytes 3538948
  20.7 18.3 %collective-permute-start.14 = (bf16[1440,256]{1,0:T(8,128)(2,1)S(1)}, bf16[1440,256]{1,0:T(8,128)(2,1)S(1)}, u32[]{:S(2)}, u32[]{:S(2)}) collective-permute-start(bf16[1440,256]{1,0:T(8,128)(2,1)S(1)} %get-tuple-element.64), channel_id=1, source_target_pairs={{0,4},{1,5},{2,6},{3,7},{4,8},{5,9},{6,10},{7,11},{8,12},{9,13},{1... | collective-permute-start | bytes 2211848 | tf_op jit(solution)/shard_map/ppermute | solution.py:21
  21.4 17.6 %collective-permute-start.15 = (bf16[1440,256]{1,0:T(8,128)(2,1)S(1)}, bf16[1440,256]{1,0:T(8,128)(2,1)S(1)}, u32[]{:S(2)}, u32[]{:S(2)}) collective-permute-start(bf16[1440,256]{1,0:T(8,128)(2,1)S(1)} %get-tuple-element.65), channel_id=1, source_target_pairs={{0,12},{1,13},{2,14},{3,15},{4,0},{5,1},{6,2},{7,3},{8,4},{9,5},{1... | collective-permute-start | bytes 2211848 | tf_op jit(solution)/shard_map/ppermute | solution.py:21
  23.5 2.8 %collective-permute-start.6 = (bf16[288,512]{1,0:T(8,128)(2,1)S(1)}, bf16[288,512]{1,0:T(8,128)(2,1)S(1)}, u32[]{:S(2)}, u32[]{:S(2)}) collective-permute-start(bf16[288,512]{1,0:T(8,128)(2,1)S(1)} %get-tuple-element.55), channel_id=1, source_target_pairs={{0,1},{1,0},{2,3},{3,2},{4,5},{5,4},{6,7},{7,6},{8,9},{9,8},{10,11... | collective-permute-start | bytes 884744 | tf_op jit(solution)/shard_map/ppermute | solution.py:21
  26.4 18.4 %collective-permute-start.11 = (bf16[576,256]{1,0:T(8,128)(2,1)S(1)}, bf16[576,256]{1,0:T(8,128)(2,1)S(1)}, u32[]{:S(2)}, u32[]{:S(2)}) collective-permute-start(bf16[576,256]{1,0:T(8,128)(2,1)S(1)} %get-tuple-element.66.block_b), channel_id=1, source_target_pairs={{0,2},{1,3},{2,0},{3,1},{4,6},{5,7},{6,4},{7,5},{8,10},{9,11},{10,... | collective-permute-start | bytes 884744 | tf_op jit(solution)/shard_map/ppermute | solution.py:21
  27.8 17.9 %collective-permute-start.12 = (bf16[576,256]{1,0:T(8,128)(2,1)S(1)}, bf16[576,256]{1,0:T(8,128)(2,1)S(1)}, u32[]{:S(2)}, u32[]{:S(2)}) collective-permute-start(bf16[576,256]{1,0:T(8,128)(2,1)S(1)} %get-tuple-element.67.block_a), channel_id=1, source_target_pairs={{0,12},{1,13},{2,14},{3,15},{4,0},{5,1},{6,2},{7,3},{8,4},{9,5},{1... | collective-permute-start | bytes 884744 | tf_op jit(solution)/shard_map/ppermute | solution.py:21
  39.0 7.8 %collective-permute-start.13 = (bf16[576,256]{1,0:T(8,128)(2,1)S(1)}, bf16[576,256]{1,0:T(8,128)(2,1)S(1)}, u32[]{:S(2)}, u32[]{:S(2)}) collective-permute-start(bf16[576,256]{1,0:T(8,128)(2,1)S(1)} %get-tuple-element.67.block_a), channel_id=1, source_target_pairs={{0,4},{1,5},{2,6},{3,7},{4,8},{5,9},{6,10},{7,11},{8,12},{9,13},{1... | collective-permute-start | bytes 884744 | tf_op jit(solution)/shard_map/ppermute | solution.py:21
  39.4 13.8 %collective-permute-start.17 = (bf16[576,256]{1,0:T(8,128)(2,1)S(1)}, bf16[576,256]{1,0:T(8,128)(2,1)S(1)}, u32[]{:S(2)}, u32[]{:S(2)}) collective-permute-start(bf16[576,256]{1,0:T(8,128)(2,1)S(1)} %get-tuple-element.73), channel_id=1, source_target_pairs={{0,4},{1,5},{2,6},{3,7},{4,8},{5,9},{6,10},{7,11},{8,12},{9,13},{1... | collective-permute-start | bytes 884744 | tf_op jit(solution)/shard_map/ppermute | solution.py:21
  39.9 13.3 %collective-permute-start.18 = (bf16[576,256]{1,0:T(8,128)(2,1)S(1)}, bf16[576,256]{1,0:T(8,128)(2,1)S(1)}, u32[]{:S(2)}, u32[]{:S(2)}) collective-permute-start(bf16[576,256]{1,0:T(8,128)(2,1)S(1)} %get-tuple-element.74), channel_id=1, source_target_pairs={{0,12},{1,13},{2,14},{3,15},{4,0},{5,1},{6,2},{7,3},{8,4},{9,5},{1... | collective-permute-start | bytes 884744 | tf_op jit(solution)/shard_map/ppermute | solution.py:21
  44.8 8.4 %collective-permute-start.19 = (bf16[576,256]{1,0:T(8,128)(2,1)S(1)}, bf16[576,256]{1,0:T(8,128)(2,1)S(1)}, u32[]{:S(2)}, u32[]{:S(2)}) collective-permute-start(bf16[576,256]{1,0:T(8,128)(2,1)S(1)} %get-tuple-element.75), channel_id=1, source_target_pairs={{0,2},{1,3},{2,0},{3,1},{4,6},{5,7},{6,4},{7,5},{8,10},{9,11},{10,... | collective-permute-start | bytes 884744 | tf_op jit(solution)/shard_map/ppermute | solution.py:21
  53.2 32.3 %collective-permute-start.25 = (bf16[3,576,256]{2,1,0:T(8,128)(2,1)}, bf16[3,576,256]{2,1,0:T(8,128)(2,1)}, u32[]{:S(2)}, u32[]{:S(2)}) collective-permute-start(bf16[3,576,256]{2,1,0:T(8,128)(2,1)} %get-tuple-element.87.along), channel_id=1, source_target_pairs={{0,2},{1,3},{2,0},{3,1},{4,6},{5,7},{6,4},{7,5},{8,10},{9,11},{10,... | collective-permute-start | bytes 2654216 | tf_op jit(solution)/shard_map/ppermute | solution.py:21
  53.3 30.8 %collective-permute-start.20 = (bf16[1440,256]{1,0:T(8,128)(2,1)}, bf16[1440,256]{1,0:T(8,128)(2,1)S(1)}, u32[]{:S(2)}, u32[]{:S(2)}) collective-permute-start(bf16[1440,256]{1,0:T(8,128)(2,1)} %get-tuple-element.76.own_up), channel_id=1, source_target_pairs={{0,4},{1,5},{2,6},{3,7},{4,8},{5,9},{6,10},{7,11},{8,12},{9,13},{1... | collective-permute-start | bytes 2211848 | tf_op jit(solution)/shard_map/ppermute | solution.py:21
  54.0 30.1 %collective-permute-start.21 = (bf16[1440,256]{1,0:T(8,128)(2,1)}, bf16[1440,256]{1,0:T(8,128)(2,1)S(1)}, u32[]{:S(2)}, u32[]{:S(2)}) collective-permute-start(bf16[1440,256]{1,0:T(8,128)(2,1)} %get-tuple-element.77), channel_id=1, source_target_pairs={{0,12},{1,13},{2,14},{3,15},{4,0},{5,1},{6,2},{7,3},{8,4},{9,5},{1... | collective-permute-start | bytes 2211848 | tf_op jit(solution)/shard_map/ppermute | solution.py:21
  56.1 0.9 copy-start.3
  57.0 5.2 %collective-permute-start.22 = (bf16[288,512]{1,0:T(8,128)(2,1)S(1)}, bf16[288,512]{1,0:T(8,128)(2,1)S(1)}, u32[]{:S(2)}, u32[]{:S(2)}) collective-permute-start(bf16[288,512]{1,0:T(8,128)(2,1)S(1)} %get-tuple-element.81), channel_id=1, source_target_pairs={{0,1},{1,0},{2,3},{3,2},{4,5},{5,4},{6,7},{7,6},{8,9},{9,8},{10,11... | collective-permute-start | bytes 884744 | tf_op jit(solution)/shard_map/ppermute | solution.py:21
  62.2 1.5 %copy-start.11 = (bf16[288,512]{1,0:T(8,128)(2,1)}, bf16[288,512]{1,0:T(8,128)(2,1)S(1)}, u32[]{:S(2)}) copy-start(bf16[288,512]{1,0:T(8,128)(2,1)S(1)} %collective-permute-done.22.other) | copy-start | bytes 884740
  62.2 27.2 %collective-permute-start.24 = (bf16[1152,256]{1,0:T(8,128)(2,1)}, bf16[1152,256]{1,0:T(8,128)(2,1)}, u32[]{:S(2)}, u32[]{:S(2)}) collective-permute-start(bf16[1152,256]{1,0:T(8,128)(2,1)} %get-tuple-element.86), channel_id=1, source_target_pairs={{0,8},{1,9},{2,10},{3,11},{4,12},{5,13},{6,14},{7,15},{8,0},{9,1},... | collective-permute-start | bytes 1769480 | tf_op jit(solution)/shard_map/ppermute | solution.py:21
  69.4 14.7 %collective-permute-start = (bf16[288,1024]{1,0:T(8,128)(2,1)}, bf16[288,1024]{1,0:T(8,128)(2,1)}, u32[]{:S(2)}, u32[]{:S(2)}) collective-permute-start(bf16[288,1024]{1,0:T(8,128)(2,1)} %param), channel_id=1, source_target_pairs={{0,16},{16,0},{32,48},{48,32},{64,80},{80,64},{96,112},{112,96},{1... | collective-permute-start | bytes 1769480 | tf_op jit(solution)/shard_map/cond/branch_0_fun/ppermute | solution.py:27
  84.1 1.5 %copy-start.2 = (bf16[3,256,1152]{2,1,0:T(8,128)(2,1)S(1)}, bf16[3,256,1152]{2,1,0:T(8,128)(2,1)}, u32[]{:S(2)}) copy-start(bf16[3,256,1152]{2,1,0:T(8,128)(2,1)} %copy-done.1) | copy-start | bytes 5308420
  84.1 6.5 %copy-start.5 = (bf16[256,1152]{1,0:T(8,128)(2,1)S(1)}, bf16[256,1152]{1,0:T(8,128)(2,1)}, u32[]{:S(2)}) copy-start(bf16[256,1152]{1,0:T(8,128)(2,1)} %copy-done.4) | copy-start | bytes 1769476
  84.1 6.5 %copy-start.7 = (bf16[256,1152]{1,0:T(8,128)(2,1)S(1)}, bf16[256,1152]{1,0:T(8,128)(2,1)}, u32[]{:S(2)}) copy-start(bf16[256,1152]{1,0:T(8,128)(2,1)} %copy-done.6) | copy-start | bytes 1769476
  84.2 6.5 %collective-permute-start.23 = (bf16[576,256]{1,0:T(8,128)(2,1)S(1)}, bf16[576,256]{1,0:T(8,128)(2,1)S(1)}, u32[]{:S(2)}, u32[]{:S(2)}) collective-permute-start(bf16[576,256]{1,0:T(8,128)(2,1)S(1)} %shard_map.102.line), channel_id=1, source_target_pairs={{0,2},{1,3},{2,0},{3,1},{4,6},{5,7},{6,4},{7,5},{8,10},{9,11},{10,... | collective-permute-start | bytes 884744 | tf_op jit(solution)/shard_map/ppermute | solution.py:21
  89.4 6.3 %copy-start.9 = (f32[288,1024]{1,0:T(8,128)S(1)}, f32[288,1024]{1,0:T(8,128)}, u32[]{:S(2)}) copy-start(f32[288,1024]{1,0:T(8,128)} %get-tuple-element.90) | copy-start | bytes 3538948
  92.5 5.5 %collective-permute-start.26 = (bf16[256,512]{1,0:T(8,128)(2,1)S(1)}, bf16[256,512]{1,0:T(8,128)(2,1)S(1)}, u32[]{:S(2)}, u32[]{:S(2)}) collective-permute-start(bf16[256,512]{1,0:T(8,128)(2,1)S(1)} %get-tuple-element.89), channel_id=1, source_target_pairs={{0,1},{1,0},{2,3},{3,2},{4,5},{5,4},{6,7},{7,6},{8,9},{9,8},{10,11... | collective-permute-start | bytes 786440 | tf_op jit(solution)/shard_map/ppermute | solution.py:21
